TPU v7x, 256 devices: a whole 4x4x8 slice. The times are simulated.
256 devices in a mesh: sec: 2 (over y_lo), dp: 16 (over x, y_hi, core), tp: 8 (over z).
Axes of the slice: x: 4, y: 4 (y_hi: 2, y_lo: 2; y = y_hi * 2 + y_lo), z: 8, core: 2. Of those that a mesh axis runs over, the one named last changes fastest.
Arguments:
- patches: bfloat16 [32, 448, 1176], P(('sec', 'dp'), 'tp'), may hold values from -6 to 6
- counts: int32 [32], replicated, may hold values from 16 to 112, as said below
- positions: int32 [32, 112], P(('sec', 'dp')), may hold values from 0 to 127, as said below
- pe_weight: bfloat16 [1176, 1280], P(None, ('sec', 'dp')), may hold values from -0.1875 to 0.1875
- ln_gain: float32 [1280], replicated, may hold values from 0.5 to 1.5
- ln_bias: float32 [1280], replicated, may hold values from -1.5 to 1.5
- w_in: bfloat16 [5120, 2560], P(None, 'tp'), may hold values from -0.078125 to 0.078125
- b_in: float32 [2560], P('tp'), may hold values from -2.5 to 2.5
- w_out: bfloat16 [2560, 8192], P('tp'), may hold values from -0.125 to 0.125
- b_out: float32 [8192], P('tp'), may hold values from -2.5 to 2.5
- text_embeds: bfloat16 [32, 128, 8192], P(('sec', 'dp'), None, 'tp'), may hold values from -6 to 6
- rms_gain: float32 [8192], P('tp'), may hold values from 0.5 to 1.5
- kv_weight: bfloat16 [8192, 2048], P(('sec', 'dp'), 'tp'), may hold values from -0.0625 to 0.0625
- kv_cotangent: bfloat16 [32, 128, 2048], P(('sec', 'dp'), None, 'tp'), may hold values from -6 to 6
Outputs:
- keys_values: bfloat16 [32, 128, 2048], P(('sec', 'dp'), None, 'tp')
- sequence_grad: bfloat16 [32, 128, 8192], P(('sec', 'dp'), None, 'tp')
- vision_grad: bfloat16 [32, 112, 8192], P(('sec', 'dp'), None, 'tp')
- kv_weight_grad: float32 [8192, 2048], P(('sec', 'dp'), 'tp')
Inputs may be any that keep to these rules, and one draw needn't show every extreme that they name: Samples pair up within each half: for every i whose remainder modulo 32/2 is below 8, counts[i] + counts[i + 8] = 128. `positions`: the 112 entries of a row are distinct.
All inputs are finite; a program needn't handle non-finite values.
Results may differ from a plain program's by a relative error of at most 0.007.
Values may be sent and summed in bfloat16 or wider, within the bound.
No kernel may reach another device: no remote copies, remote signals or barrier semaphores. Data moves between devices by JAX's collectives and lax.ppermute only.
A program may use at most 64 MiB of HBM per device.

v0:
```python
import jax
import jax.numpy as jnp
from jax import lax
from jax.sharding import PartitionSpec as P

WIDTH = 8192
MERGE_PATCHES = 4


def partner(block, axis, bit):
    count = lax.axis_size(axis)
    route = []
    for low in range(count):
        high = low | 1 << bit
        if high != low and high < count:
            route += [(low, high), (high, low)]
    return lax.ppermute(block, axis, route)


def layer_norm(values, gain_vector, bias_vector):
    average = jnp.mean(values, axis=-1, keepdims=True)
    centered = values - average
    variance = jnp.mean(centered * centered, axis=-1, keepdims=True)
    return centered * lax.rsqrt(variance + 1e-06) * gain_vector + bias_vector


def per_device(
    patches,
    counts,
    positions,
    pe_weight,
    ln_gain,
    ln_bias,
    w_in,
    b_in,
    w_out,
    b_out,
    text_embeds,
    rms_gain,
    kv_weight,
    kv_cotangent,
):
    dp_size = lax.axis_size("dp")
    sample = lax.axis_index("sec") * dp_size + lax.axis_index("dp")
    image_count = counts[(sample + dp_size) % (2 * dp_size)]
    full_patch = lax.all_gather(pe_weight, ("sec", "dp"), axis=1, tiled=True)
    projected = jnp.dot(patches[0], full_patch, preferred_element_type=jnp.float32)
    embedded = layer_norm(projected, ln_gain, ln_bias).astype(jnp.bfloat16)
    patch_all = lax.all_gather(embedded, "tp", axis=0, tiled=True)
    merged = patch_all.reshape(patch_all.shape[0] // MERGE_PATCHES, -1)
    before_gelu = jnp.dot(merged, w_in, preferred_element_type=jnp.float32) + b_in
    hidden = jax.nn.gelu(before_gelu, approximate=False).astype(jnp.bfloat16)
    summed = lax.psum_scatter(
        lax.dot_general(
            w_out, hidden, (((0,), (1,)), ((), ())), preferred_element_type=jnp.float32
        ),
        "tp",
        scatter_dimension=0,
        tiled=True,
    )
    vision = (summed.T + b_out).astype(jnp.bfloat16)
    arrived = partner(vision, "sec", 0)
    text_rows = text_embeds[0]
    slot_positions = positions[0]
    slot_index = jnp.arange(slot_positions.shape[0])
    line_index = jnp.arange(text_rows.shape[0])
    selector = (slot_positions[None, :] == line_index[:, None]) & (
        slot_index[None, :] < image_count
    )
    selector_bf = selector.astype(jnp.bfloat16)
    placed = jnp.dot(selector_bf, arrived, preferred_element_type=jnp.float32)
    image_rows = jnp.any(selector, axis=1, keepdims=True)
    combined = jnp.where(image_rows, placed, text_rows.astype(jnp.float32))
    row_squares = lax.psum(jnp.sum(combined * combined, axis=1), "tp")
    row_scale = lax.rsqrt(row_squares / WIDTH + 1e-06)[:, None]
    normed = (combined * row_scale * rms_gain).astype(jnp.bfloat16)
    full_weight = lax.all_gather(kv_weight, ("sec", "dp"), axis=0, tiled=True)
    normed_full = lax.all_gather(normed, "tp", axis=1, tiled=True)
    keys_values = jnp.dot(normed_full, full_weight, preferred_element_type=jnp.float32).astype(
        jnp.bfloat16
    )
    cotangent = kv_cotangent[0]
    partial_grad = lax.dot_general(
        cotangent, full_weight, (((1,), (1,)), ((), ())), preferred_element_type=jnp.float32
    )
    normed_grad = lax.psum_scatter(partial_grad, "tp", scatter_dimension=1, tiled=True)
    scaled = normed_grad * rms_gain
    row_dot = lax.psum(jnp.sum(scaled * combined, axis=1), "tp")[:, None]
    seq_grad = (
        row_scale * scaled - combined * row_scale * row_scale * row_scale * row_dot / WIDTH
    ).astype(jnp.bfloat16)
    image_grad = lax.dot_general(
        selector_bf, seq_grad, (((0,), (0,)), ((), ())), preferred_element_type=jnp.float32
    ).astype(jnp.bfloat16)
    vision_grad = partner(image_grad, "sec", 0)
    kv_weight_grad = lax.psum_scatter(
        lax.dot_general(
            normed_full, cotangent, (((0,), (0,)), ((), ())), preferred_element_type=jnp.float32
        ),
        ("sec", "dp"),
        scatter_dimension=0,
        tiled=True,
    )
    return (keys_values[None], seq_grad[None], vision_grad[None], kv_weight_grad)


def solution(mesh):
    return jax.shard_map(
        per_device,
        mesh=mesh,
        in_specs=(
            P(("sec", "dp"), "tp", None),
            P(),
            P(("sec", "dp"), None),
            P(None, ("sec", "dp")),
            P(),
            P(),
            P(None, "tp"),
            P("tp"),
            P("tp", None),
            P("tp"),
            P(("sec", "dp"), None, "tp"),
            P("tp"),
            P(("sec", "dp"), "tp"),
            P(("sec", "dp"), None, "tp"),
        ),
        out_specs=(
            P(("sec", "dp"), None, "tp"),
            P(("sec", "dp"), None, "tp"),
            P(("sec", "dp"), None, "tp"),
            P(("sec", "dp"), "tp"),
        ),
        check_vma=False,
    )
```

profile of v0, /device:TPU:14, one launch (start us, length us, event | category | flops | bytes accessed | tf_op | source)
XLA Modules:
  0.0 507.2 jit_solution(12768386549643400316)
XLA Ops:
  7.2 0.0 copy-start
  7.2 0.0 copy-start.5
  7.2 0.0 all-gather.5.cloned.1.call-start
  7.2 0.7 all-gather.5.cloned.1.call-update
  7.9 0.0 all-gather.7.cloned.1.call-start
  8.0 64.5 %all-gather.5.cloned.1.call-done = bf16[1176,1280]{0,1:T(8,128)(2,1)} async-done(((bf16[1176,40]{0,1:T(8,128)(2,1)}), bf16[1176,1280]{0,1:T(8,128)(2,1)}) %all-gather.5.cloned.1.call-update) | async-done | bytes 3010576 | tf_op jit(solution)/shard_map/all_gather | solution.py:46
  72.5 3.2 fusion.87
  75.7 0.2 multiply_reduce_fusion.2
  76.0 0.8 add_convert_fusion.1
  76.7 0.0 all-gather.7.cloned.1.call-update
  76.8 0.0 all-gather.11.cloned.1.call-start
  76.8 0.7 all-gather.11.cloned.1.call-update
  77.5 0.0 reduce-scatter.4.cloned.1.call-start
  77.5 39.1 %all-gather.7.cloned.1.call-done = bf16[448,1280]{1,0:T(8,128)(2,1)} async-done(((bf16[56,1280]{1,0:T(8,128)(2,1)}), bf16[448,1280]{1,0:T(8,128)(2,1)}) %all-gather.7.cloned.1.call-update) | async-done | bytes 1146896 | tf_op jit(solution)/shard_map/all_gather | solution.py:49
  116.7 2.6 reshape.38
  119.3 7.2 %convolution_bitcast_fusion = f32[8192,112]{0,1:T(8,128)} fusion(bf16[320,8192]{1,0:T(8,128)(2,1)} %param.22, bf16[112,5120]{1,0:T(8,128)(2,1)} %reshape.38, bf16[5120,320]{0,1:T(8,128)(2,1)S(1)} %copy-done, f32[320]{0:T(512)S(1)} %copy-done.9), kind=kOutput, calls=%fused_computation | convolution fusion | flops 956569600 | bytes 13337856 | tf_op jit(solution)/shard_map/dot_general | solution.py:54
  126.5 0.0 reduce-scatter.4.cloned.1.call-update
  126.5 0.0 reduce-scatter.6.cloned.1.call-start
  126.6 51.8 %all-gather.11.cloned.1.call-done = bf16[8192,256]{1,0:T(8,128)(2,1)} async-done(((bf16[256,256]{1,0:T(8,128)(2,1)}), bf16[8192,256]{1,0:T(8,128)(2,1)}) %all-gather.11.cloned.1.call-update) | async-done | bytes 4194320 | tf_op jit(solution)/shard_map/all_gather | solution.py:77
  178.4 0.0 copy-done.2
  178.4 5.6 %fusion.47 = f32[128,8192]{1,0:T(8,128)} fusion(bf16[8192,256]{1,0:T(8,128)(2,1)} %all-gather.11.cloned.1.call-done, bf16[1,128,256]{2,1,0:T(8,128)(2,1)S(1)} %copy-done.2), kind=kOutput, calls=%fused_computation.68 | convolution fusion | flops 536870912 | bytes 8454144 | tf_op jit(solution)/shard_map/dot_general | solution.py:83
  184.0 0.0 copy-start.4
  184.0 0.0 reduce-scatter.6.cloned.1.call-update
  184.0 0.0 all-gather.9.cloned.1.call-start
  184.1 48.0 %reduce-scatter.4.cloned.1.call-done = f32[1024,112]{0,1:T(8,128)} async-done(((f32[8192,112]{0,1:T(8,128)}), f32[1024,112]{0,1:T(8,128)}) %reduce-scatter.4.cloned.1.call-update) | async-done | bytes 458768 | tf_op jit(solution)/shard_map/reduce_scatter | solution.py:53
  232.1 0.0 copy-done.7
  232.1 1.7 fusion.1
  233.8 0.5 collective-permute-start
  234.4 0.6 dynamic_slice.3
  235.0 0.6 iota_compare_fusion.1
  235.6 0.1 fusion.52
  235.7 5.8 %collective-permute-done = bf16[112,1024]{1,0:T(8,128)(2,1)} collective-permute-done((bf16[112,1024]{1,0:T(8,128)(2,1)}, bf16[112,1024]{1,0:T(8,128)(2,1)}, u32[]{:S(2)}, u32[]{:S(2)}) %collective-permute-start) | collective-permute-done | bytes 229408 | tf_op jit(solution)/shard_map/ppermute | solution.py:17
  241.6 47.3 %reduce-scatter.6.cloned.1.call-done = f32[128,1024]{1,0:T(8,128)} async-done(((f32[128,8192]{1,0:T(8,128)}), f32[128,1024]{1,0:T(8,128)}) %reduce-scatter.6.cloned.1.call-update) | async-done | bytes 524304 | tf_op jit(solution)/shard_map/reduce_scatter | solution.py:86
  288.8 0.0 copy-done.3
  288.8 2.8 multiply_reduce_fusion
  291.7 15.6 %all-reduce = (f32[128]{0:T(128)S(1)}, f32[128]{0:T(128)S(1)}) all-reduce(f32[128]{0:T(128)} %get-tuple-element.5, f32[128]{0:T(128)} %get-tuple-element.4), channel_id=1, replica_groups=mesh['sec'=2,'dp'=16,'tp'=8] {'tp'}, use_global_device_ids=true, to_apply=%region_5.6 | all-reduce | flops 256 | bytes 2048 | tf_op jit(solution)/shard_map/psum | solution.py:74
  307.3 2.1 subtract_convert_fusion
  309.4 0.0 all-gather.9.cloned.1.call-update
  309.5 0.0 reduce-scatter.8.cloned.1.call-start
  309.5 41.1 %all-gather.9.cloned.1.call-done = bf16[128,8192]{1,0:T(8,128)(2,1)} async-done(((bf16[128,1024]{1,0:T(8,128)(2,1)}), bf16[128,8192]{1,0:T(8,128)(2,1)}) %all-gather.9.cloned.1.call-update) | async-done | bytes 2097168 | tf_op jit(solution)/shard_map/all_gather | solution.py:78
  350.6 6.1 %fusion.45 = f32[8192,256]{1,0:T(8,128)} fusion(bf16[128,8192]{1,0:T(8,128)(2,1)} %all-gather.9.cloned.1.call-done, bf16[1,128,256]{2,1,0:T(8,128)(2,1)} %param.27), kind=kOutput, calls=%fused_computation.66 | convolution fusion | flops 536870912 | bytes 10551296 | tf_op jit(solution)/shard_map/dot_general | solution.py:97
  356.7 0.0 reduce-scatter.8.cloned.1.call-update
  356.7 0.3 convolution_convert_fusion
  357.0 0.6 collective-permute-start.1
  357.6 5.5 %collective-permute-done.1 = bf16[112,1024]{1,0:T(8,128)(2,1)S(1)} collective-permute-done((bf16[112,1024]{1,0:T(8,128)(2,1)S(1)}, bf16[112,1024]{1,0:T(8,128)(2,1)S(1)}, u32[]{:S(2)}, u32[]{:S(2)}) %collective-permute-start.1) | collective-permute-done | bytes 229408 | tf_op jit(solution)/shard_map/ppermute | solution.py:17
  363.1 4.2 fusion
  367.2 132.4 %reduce-scatter.8.cloned.1.call-done = f32[256,256]{1,0:T(8,128)} async-done(((f32[8192,256]{1,0:T(8,128)}), f32[256,256]{1,0:T(8,128)}) %reduce-scatter.8.cloned.1.call-update) | async-done | bytes 262160 | tf_op jit(solution)/shard_map/reduce_scatter | solution.py:96
  499.6 0.7 copy.19
  (19 shorter events, 0.1 us)
Async XLA Ops:
  7.2 112.1 %copy-start = (bf16[5120,320]{0,1:T(8,128)(2,1)S(1)}, bf16[5120,320]{0,1:T(8,128)(2,1)}, u32[]{:S(2)}) copy-start(bf16[5120,320]{0,1:T(8,128)(2,1)} %param.20) | copy-start | bytes 9830404
  7.2 68.8 %copy-start.5 = (f32[1280]{0:T(1024)S(1)}, f32[1280]{0:T(1024)}, u32[]{:S(2)}) copy-start(f32[1280]{0:T(1024)} %param.19) | copy-start | bytes 15364
  7.2 68.8 %copy-start.6 = (f32[1280]{0:T(1024)S(1)}, f32[1280]{0:T(1024)}, u32[]{:S(2)}) copy-start(f32[1280]{0:T(1024)} %param.18) | copy-start | bytes 15364
  7.2 65.3 %all-gather.5.cloned.1.call-start = ((), (), s32[]{:S(2)}) async-start(), calls=%async_computation.3 | async-start | bytes 3379200 | tf_op jit(solution)/shard_map/all_gather | solution.py:46
  7.9 111.4 %copy-start.9 = (f32[320]{0:T(512)S(1)}, f32[320]{0:T(512)}, u32[]{:S(2)}) copy-start(f32[320]{0:T(512)} %param.21) | copy-start | bytes 3844
  7.9 108.7 %all-gather.7.cloned.1.call-start = ((), (), s32[]{:S(2)}) async-start(), calls=%async_computation.4 | async-start | bytes 1290240 | tf_op jit(solution)/shard_map/all_gather | solution.py:49
  76.8 101.6 %all-gather.11.cloned.1.call-start = ((), (), s32[]{:S(2)}) async-start(), calls=%async_computation.7 | async-start | bytes 4325376 | tf_op jit(solution)/shard_map/all_gather | solution.py:77
  77.5 154.6 %reduce-scatter.4.cloned.1.call-start = ((), (), s32[]{:S(2)}) async-start(), calls=%async_computation.5 | async-start | bytes 4128768 | tf_op jit(solution)/shard_map/reduce_scatter | solution.py:53
  126.5 51.9 %copy-start.2 = (bf16[1,128,256]{2,1,0:T(8,128)(2,1)S(1)}, bf16[1,128,256]{2,1,0:T(8,128)(2,1)}, u32[]{:S(2)}) copy-start(bf16[1,128,256]{2,1,0:T(8,128)(2,1)} %param.27) | copy-start | bytes 196612
  126.5 162.3 %reduce-scatter.6.cloned.1.call-start = ((), (), s32[]{:S(2)}) async-start(), calls=%async_computation.8 | async-start | bytes 4718592 | tf_op jit(solution)/shard_map/reduce_scatter | solution.py:86
  184.0 48.1 %copy-start.7 = (f32[1024]{0:T(1024)S(1)}, f32[1024]{0:T(1024)}, u32[]{:S(2)}) copy-start(f32[1024]{0:T(1024)} %param.23) | copy-start | bytes 12292
  184.0 50.4 %copy-start.10 = (s32[32]{0:T(128)S(1)}, s32[32]{0:T(128)}, u32[]{:S(2)}) copy-start(s32[32]{0:T(128)} %param.15) | copy-start | bytes 388
  184.0 51.6 %copy-start.8 = (s32[1,112]{1,0:T(1,128)S(1)}, s32[1,112]{1,0:T(1,128)}, u32[]{:S(2)}) copy-start(s32[1,112]{1,0:T(1,128)} %param.16) | copy-start | bytes 1348
  184.0 104.8 %copy-start.3 = (bf16[1,128,1024]{2,1,0:T(8,128)(2,1)S(1)}, bf16[1,128,1024]{2,1,0:T(8,128)(2,1)}, u32[]{:S(2)}) copy-start(bf16[1,128,1024]{2,1,0:T(8,128)(2,1)} %param.24) | copy-start | bytes 786436
  184.0 104.8 %copy-start.4 = (f32[1024]{0:T(1024)S(1)}, f32[1024]{0:T(1024)}, u32[]{:S(2)}) copy-start(f32[1024]{0:T(1024)} %param.25) | copy-start | bytes 12292
  184.0 166.5 %all-gather.9.cloned.1.call-start = ((), (), s32[]{:S(2)}) async-start(), calls=%async_computation.6 | async-start | bytes 2359296 | tf_op jit(solution)/shard_map/all_gather | solution.py:78
  233.8 7.7 %collective-permute-start = (bf16[112,1024]{1,0:T(8,128)(2,1)}, bf16[112,1024]{1,0:T(8,128)(2,1)}, u32[]{:S(2)}, u32[]{:S(2)}) collective-permute-start(bf16[112,1024]{1,0:T(8,128)(2,1)} %fusion.1), channel_id=1, source_target_pairs={{0,128},{128,0},{1,129},{129,1},{2,130},{130,2},{3,131},{131,3},{4... | collective-permute-start | bytes 688136 | tf_op jit(solution)/shard_map/ppermute | solution.py:17
  309.4 47.3 %copy-start.1 = (bf16[128,1024]{1,0:T(8,128)(2,1)}, bf16[128,1024]{1,0:T(8,128)(2,1)S(1)}, u32[]{:S(2)}) copy-start(bf16[128,1024]{1,0:T(8,128)(2,1)S(1)} %get-tuple-element.8) | copy-start | bytes 786436
  309.5 190.2 %reduce-scatter.8.cloned.1.call-start = ((), (), s32[]{:S(2)}) async-start(), calls=%async_computation.9 | async-start | bytes 8650752 | tf_op jit(solution)/shard_map/reduce_scatter | solution.py:96
  357.0 6.1 %collective-permute-start.1 = (bf16[112,1024]{1,0:T(8,128)(2,1)S(1)}, bf16[112,1024]{1,0:T(8,128)(2,1)S(1)}, u32[]{:S(2)}, u32[]{:S(2)}) collective-permute-start(bf16[112,1024]{1,0:T(8,128)(2,1)S(1)} %convolution_convert_fusion), channel_id=1, source_target_pairs={{0,128},{128,0},{1,129},{129,1},{2,130},{130,2},{3,131},{131,3},{4... | collective-permute-start | bytes 688136 | tf_op jit(solution)/shard_map/ppermute | solution.py:17
Sparse Core Ops, SparseCore 0:
  9.9 62.5 all-gather.4
  76.9 39.7 all-gather.6
  118.5 59.7 all-gather.10
  180.8 51.2 reduce-scatter.3
  234.5 54.2 reduce-scatter.5
  309.6 40.9 all-gather.8
  356.8 142.7 reduce-scatter.7
where the time goes:
time: 516 us; the launch traced here: 507 us
  waiting for transfers between devices  437 us (85%)
  matrix products  29.4 us (6%)
  blocking collectives  15.6 us (3%)
  between operations  14.2 us (3%)
  other arithmetic  5.64 us (1%)
    reduce_scatter x1, waiting for transfers between devices, per_device(): lax.psum_scatter(lax.dot_general(normed_full, cotangent, (((0,), (0,)), (...  132 us
    all_gather x1, waiting for transfers between devices, per_device(): full_patch = lax.all_gather(pe_weight, ('sec', 'dp'), axis=1, tiled=True)  64.5 us
    all_gather x1, waiting for transfers between devices, per_device(): full_weight = lax.all_gather(kv_weight, ('sec', 'dp'), axis=0, tiled=True)  51.8 us
    reduce_scatter x1, waiting for transfers between devices, per_device(): lax.psum_scatter(lax.dot_general(w_out, hidden, (((0,), (1,)), ((), ())),...  48 us
    reduce_scatter x1, waiting for transfers between devices, per_device(): lax.psum_scatter(partial_grad, 'tp', scatter_dimension=1, tiled=True)  47.3 us
    all_gather x1, waiting for transfers between devices, per_device(): normed_full = lax.all_gather(normed, 'tp', axis=1, tiled=True)  41.1 us
    all_gather x1, waiting for transfers between devices, per_device(): patch_all = lax.all_gather(embedded, 'tp', axis=0, tiled=True)  39.1 us
    psum x1, blocking collectives, per_device(): row_squares = lax.psum(jnp.sum(combined * combined, axis=1), 'tp')  15.6 us
  transfers between devices with their start and end apart: 9, of which 9 were waited for; matrix products, arithmetic and copies ran while one was open for 5% of the time, Pallas kernels for 0%

commit v1 on v0

v1 whole, which is shorter than its diff:
```python
import jax
import jax.numpy as jnp
from jax import lax
from jax.experimental import pallas as pl
from jax.sharding import PartitionSpec as P

WIDTH = 8192
MERGE_PATCHES = 4
PLANE = ("sec", "dp")
ALL = ("sec", "dp", "tp")
N_TP = 8
BF = jnp.bfloat16
F32 = jnp.float32


def plane_index(x, y, core):
    return (y % 2) * 16 + x * 4 + (y // 2) * 2 + core


SAME_CORE = [
    [plane_index(x, y, core) for lo in range(2) for x in range(4) for y in (lo, lo + 2)]
    for core in range(2)
]
SAME_X = [[plane_index(x, y, core) for y in range(4)] for x in range(4) for core in range(2)]
SAME_Y = [[plane_index(x, y, core) for x in range(4)] for y in range(4) for core in range(2)]


def swap_cores(block):
    return lax.ppermute(block, "dp", [(i, i ^ 1) for i in range(16)])


def swap_halves(block):
    return lax.ppermute(block, "sec", [(0, 1), (1, 0)])


def weight_to_plane():
    route = []
    for p in range(32):
        for t in range(N_TP):
            route.append((p * N_TP + t, (t * 4 + p % 4) * N_TP + p // 4))
    return route


def grad_from_plane():
    route = []
    for x in range(4):
        for y in range(4):
            for core in range(2):
                for t in range(N_TP):
                    source = plane_index(x, y, core) * N_TP + t
                    row = 4 * t + 2 * core + x // 2
                    route.append((source, row * N_TP + ((2 * y + x % 2) ^ t)))
    return route


def column_product_kernel(left_ref, right_ref, out_ref):
    out_ref[0] = jnp.dot(
        left_ref[...], right_ref[...], preferred_element_type=F32
    ).astype(out_ref.dtype)


def column_product(left, right):
    rows, depth = left.shape
    width = right.shape[1] // N_TP
    return pl.pallas_call(
        column_product_kernel,
        grid=(N_TP,),
        in_specs=[
            pl.BlockSpec((rows, depth), lambda i: (0, 0)),
            pl.BlockSpec((depth, width), lambda i: (0, i)),
        ],
        out_specs=pl.BlockSpec((1, rows, width), lambda i: (i, 0, 0)),
        out_shape=jax.ShapeDtypeStruct((N_TP, rows, width), BF),
        cost_estimate=pl.CostEstimate(
            flops=2 * rows * right.size, bytes_accessed=2 * right.size, transcendentals=0
        ),
    )(left, right)


def block_product_kernel(left_ref, right_ref, out_ref):
    out_ref[0] = jnp.dot(
        left_ref[...], right_ref[0], preferred_element_type=F32
    ).astype(out_ref.dtype)


def block_product(left, right):
    rows, depth = left.shape
    width = right.shape[2]
    return pl.pallas_call(
        block_product_kernel,
        grid=(N_TP,),
        in_specs=[
            pl.BlockSpec((rows, depth), lambda i: (0, 0)),
            pl.BlockSpec((1, depth, width), lambda i: (i, 0, 0)),
        ],
        out_specs=pl.BlockSpec((1, rows, width), lambda i: (i, 0, 0)),
        out_shape=jax.ShapeDtypeStruct((N_TP, rows, width), BF),
        cost_estimate=pl.CostEstimate(
            flops=2 * rows * right.size, bytes_accessed=2 * right.size, transcendentals=0
        ),
    )(left, right)


def block_sum_kernel(left_ref, right_ref, out_ref):
    part = lax.dot_general(
        left_ref[0], right_ref[0], (((1,), (1,)), ((), ())), preferred_element_type=F32
    )

    @pl.when(pl.program_id(0) == 0)
    def _():
        out_ref[...] = part

    @pl.when(pl.program_id(0) > 0)
    def _():
        out_ref[...] += part


def block_sum(left, right):
    rows, width = left.shape[1:]
    depth = right.shape[1]
    return pl.pallas_call(
        block_sum_kernel,
        grid=(N_TP,),
        in_specs=[
            pl.BlockSpec((1, rows, width), lambda i: (i, 0, 0)),
            pl.BlockSpec((1, depth, width), lambda i: (i, 0, 0)),
        ],
        out_specs=pl.BlockSpec((rows, depth), lambda i: (0, 0)),
        out_shape=jax.ShapeDtypeStruct((rows, depth), F32),
        cost_estimate=pl.CostEstimate(
            flops=2 * rows * right.size, bytes_accessed=2 * right.size, transcendentals=0
        ),
    )(left, right)


def line_product_kernel(normed_ref, own_ref, other_ref, out_ref):
    total = jnp.zeros((512, 512), F32)
    for side, cot_ref in enumerate((own_ref, other_ref)):
        total += lax.dot_general(
            normed_ref[:, side].reshape(512, 512),
            cot_ref[...].reshape(512, 512),
            (((0,), (0,)), ((), ())),
            preferred_element_type=F32,
        )
    for i in range(4):
        row, col = i // 2 * 256, i % 2 * 256
        out_ref[i] = total[row : row + 256, col : col + 256].astype(BF)


def line_product(normed, own, other):
    return pl.pallas_call(
        line_product_kernel,
        out_shape=jax.ShapeDtypeStruct((4, 256, 256), BF),
        cost_estimate=pl.CostEstimate(
            flops=2 * 1024 * 512 * 512, bytes_accessed=3 << 20, transcendentals=0
        ),
    )(normed, own, other)


def flip_bits(blocks, number):
    shape = blocks.shape
    blocks = blocks.reshape((2, 2, 2) + shape[1:])
    for axis in range(3):
        bit = (number >> (2 - axis)) & 1
        blocks = jnp.where(bit == 1, jnp.flip(blocks, axis), blocks)
    return blocks.reshape(shape)


def layer_norm(values, gain_vector, bias_vector):
    average = jnp.mean(values, axis=-1, keepdims=True)
    centered = values - average
    variance = jnp.mean(centered * centered, axis=-1, keepdims=True)
    return centered * lax.rsqrt(variance + 1e-06) * gain_vector + bias_vector


def exchange_tp(blocks):
    return lax.all_to_all(blocks, "tp", 0, 0)


def gather_tp(block):
    return exchange_tp(jnp.broadcast_to(block[None], (N_TP,) + block.shape))


def per_device(
    patches,
    counts,
    positions,
    pe_weight,
    ln_gain,
    ln_bias,
    w_in,
    b_in,
    w_out,
    b_out,
    text_embeds,
    rms_gain,
    kv_weight,
    kv_cotangent,
):
    sec = lax.axis_index("sec")
    dp = lax.axis_index("dp")
    tp = lax.axis_index("tp")
    core = dp % 2
    image_count = counts[(1 - sec) * 16 + dp]

    tokens = patches.shape[1] // MERGE_PATCHES
    rows = patches[0].reshape(tokens, MERGE_PATCHES, -1).transpose(1, 0, 2)
    rows = jnp.pad(rows, ((0, 0), (0, 16 - tokens), (0, 0))).reshape(MERGE_PATCHES * 16, -1)
    columns, rows = lax.optimization_barrier((pe_weight.T, rows))
    patch_all = lax.all_gather(rows, "tp", tiled=True)

    mine = lax.all_to_all(
        jnp.broadcast_to(columns[None], (16,) + columns.shape),
        PLANE,
        0,
        0,
        axis_index_groups=SAME_CORE,
    )
    other = swap_cores(mine)
    first = jnp.where(core == 0, mine, other)
    second = jnp.where(core == 0, other, mine)
    full_patch = jnp.stack([first, second], axis=1).reshape(1280, -1)

    weight_block = lax.ppermute(kv_weight, ALL, weight_to_plane())
    weight_block, cot_input, _ = lax.optimization_barrier((weight_block, kv_cotangent[0], mine))
    weight_all = lax.all_gather(weight_block, PLANE).reshape(N_TP, 1024, 256)

    cotangents = gather_tp(cot_input)
    cot_line = flip_bits(cotangents, tp)
    cot_line = cot_line.reshape(4, 2, 128, 256).transpose(0, 2, 1, 3).reshape(4, 128, 512)
    projected = lax.dot_general(
        patch_all, full_patch, (((1,), (1,)), ((), ())), preferred_element_type=F32
    )
    cot_line, projected = lax.optimization_barrier((cot_line, projected))
    cot_line = lax.all_to_all(cot_line, PLANE, 0, 0, axis_index_groups=SAME_X)
    cot_other = swap_cores(cot_line)

    embedded = layer_norm(projected, ln_gain, ln_bias).astype(BF)
    embedded = embedded.reshape(N_TP, MERGE_PATCHES, 16, 1280)
    merged = jnp.concatenate(
        [embedded[:, m].reshape(N_TP * 16, 1280) for m in range(MERGE_PATCHES)], axis=1
    )
    before_gelu = jnp.dot(merged, w_in, preferred_element_type=F32) + b_in
    hidden = jax.nn.gelu(before_gelu, approximate=False).astype(BF)
    hidden = hidden.reshape(N_TP, 16, -1)[:, :tokens].reshape(N_TP * tokens, -1)
    hidden = swap_halves(hidden)
    hidden, cot_line, cot_other = lax.optimization_barrier((hidden, cot_line, cot_other))
    partial = column_product(hidden, w_out)
    vision = (jnp.sum(exchange_tp(partial).astype(F32), axis=0) + b_out).astype(BF)

    line_index = jnp.arange(128)
    slot_positions = positions[0]
    slot_ok = jnp.arange(112) < image_count
    selector = (slot_positions[None, :] == line_index[:, None]) & slot_ok[None, :]
    selector_bf = selector.astype(BF)
    placed = jnp.dot(selector_bf, vision, preferred_element_type=F32)
    image_rows = jnp.any(selector, axis=1, keepdims=True)
    combined = jnp.where(image_rows, placed, text_embeds[0].astype(F32))

    normed_grad = block_sum(cotangents, weight_all)
    scaled = normed_grad * rms_gain
    stats = jnp.stack([jnp.sum(combined * combined, axis=1), jnp.sum(scaled * combined, axis=1)])
    stats = jnp.sum(gather_tp(stats), axis=0)
    row_scale = lax.rsqrt(stats[0] / WIDTH + 1e-06)[:, None]
    row_dot = stats[1][:, None]
    seq_grad = (
        row_scale * scaled - combined * row_scale * row_scale * row_scale * row_dot / WIDTH
    ).astype(BF)
    image_grad = lax.dot_general(
        selector_bf, seq_grad, (((0,), (0,)), ((), ())), preferred_element_type=F32
    ).astype(BF)
    vision_grad = swap_halves(image_grad)

    gained = combined * rms_gain
    normed = (gained * row_scale).astype(BF)
    keep = jnp.where(core == 0, normed[:, :512], normed[:, 512:])
    give = jnp.where(core == 0, normed[:, 512:], normed[:, :512])
    pair = jnp.stack([keep, swap_cores(give)])
    normed_line = lax.all_to_all(
        jnp.broadcast_to(pair[None], (4,) + pair.shape), PLANE, 0, 0, axis_index_groups=SAME_X
    )
    block = line_product(normed_line, cot_line, cot_other)
    block = lax.all_to_all(block, PLANE, 0, 0, axis_index_groups=SAME_Y)
    block = jnp.sum(block.astype(F32), axis=0).astype(BF)
    kv_weight_grad = lax.ppermute(block, ALL, grad_from_plane()).astype(F32)

    product = block_product(gained.astype(BF), weight_all)
    keys_values = jnp.sum(exchange_tp(product).astype(F32), axis=0)
    keys_values = (keys_values * row_scale).astype(BF)
    return (keys_values[None], seq_grad[None], vision_grad[None], kv_weight_grad)


def solution(mesh):
    return jax.shard_map(
        per_device,
        mesh=mesh,
        in_specs=(
            P(("sec", "dp"), "tp", None),
            P(),
            P(("sec", "dp"), None),
            P(None, ("sec", "dp")),
            P(),
            P(),
            P(None, "tp"),
            P("tp"),
            P("tp", None),
            P("tp"),
            P(("sec", "dp"), None, "tp"),
            P("tp"),
            P(("sec", "dp"), "tp"),
            P(("sec", "dp"), None, "tp"),
        ),
        out_specs=(
            P(("sec", "dp"), None, "tp"),
            P(("sec", "dp"), None, "tp"),
            P(("sec", "dp"), None, "tp"),
            P(("sec", "dp"), "tp"),
        ),
        check_vma=False,
    )
```

time: 516 us -> 283 us (0.55); the launches traced: 507 us -> 281 us
  waiting for transfers between devices: 437 us -> 130 us
  starting transfers between devices: 1.46 us -> 56.2 us
  Pallas kernels: 0 us -> 24 us
  matrix products: 29.4 us -> 11 us
  other arithmetic: 5.64 us -> 20.4 us
  local copies, waits for them, and re-layouts: 3.91 us -> 14.5 us
  blocking collectives: 15.6 us -> 10.1 us
    reduce_scatter x3 -> x0, waiting for transfers between devices: 228 us -> none  [the longest x1 132 us: per_device(): lax.psum_scatter(lax.dot_general(normed_full, cotangent, (((0,), (0,)), (...]
    all_gather x4 -> x2, waiting for transfers between devices: 196 us -> 0.01 us  [the longest x1 0.01 us: per_device(): patch_all = lax.all_gather(rows, 'tp', tiled=True)]
    all_to_all x0 -> x7, waiting for transfers between devices: none -> 92.3 us  [the longest x3 74.4 us: exchange_tp(): return lax.all_to_all(blocks, 'tp', 0, 0)]
    all_to_all x0 -> x7, starting transfers between devices: none -> 44.6 us  [the longest x3 21.3 us: exchange_tp(): return lax.all_to_all(blocks, 'tp', 0, 0)]
    ppermute x2 -> x7, waiting for transfers between devices: 11.3 us -> 36.6 us  [the longest x1 12.3 us: per_device(): kv_weight_grad = lax.ppermute(block, ALL, grad_from_plane()).astype(F32)]
    pallas_call x0 -> x4, Pallas kernels: none -> 24 us  [the longest x1 7.29 us: column_product(): pl.pallas_call(column_product_kernel, grid=(N_TP,), in_specs=[pl.BlockSpe...]
    dot_general x6 -> x3, matrix products: 29.2 us -> 10.7 us  [the longest x1 5.78 us: per_device(): lax.dot_general(patch_all, full_patch, (((1,), (1,)), ((), ())), preferre...]
    psum x1 -> x0, blocking collectives: 15.6 us -> none  [per_device(): row_squares = lax.psum(jnp.sum(combined * combined, axis=1), 'tp')]
  transfers between devices with their start and end apart: 9 -> 16, of which waited for: 9 -> 11; matrix products, arithmetic and copies ran while one was open for 5% -> 11% of each run, Pallas kernels for 0% -> 6%
where the time goes in v1:
time: 283 us; the launch traced here: 281 us
  waiting for transfers between devices  130 us (46%)
  starting transfers between devices  56.2 us (20%)
  Pallas kernels  24 us (8%)
  other arithmetic  20.4 us (7%)
  local copies, waits for them, and re-layouts  14.5 us (5%)
  between operations  14.3 us (5%)
  matrix products  11 us (4%)
  blocking collectives  10.1 us (4%)
    all_to_all x3, waiting for transfers between devices, exchange_tp(): return lax.all_to_all(blocks, 'tp', 0, 0)  74.4 us
    all_to_all x3, starting transfers between devices, exchange_tp(): return lax.all_to_all(blocks, 'tp', 0, 0)  21.3 us
    ppermute x1, waiting for transfers between devices, per_device(): kv_weight_grad = lax.ppermute(block, ALL, grad_from_plane()).astype(F32)  12.3 us
    ppermute x1, waiting for transfers between devices, per_device(): weight_block = lax.ppermute(kv_weight, ALL, weight_to_plane())  12.2 us
    ppermute x2, waiting for transfers between devices, swap_halves(): return lax.ppermute(block, 'sec', [(0, 1), (1, 0)])  10.7 us
    all_to_all x1, blocking collectives, exchange_tp(): return lax.all_to_all(blocks, 'tp', 0, 0)  10.1 us
    all_to_all x1, waiting for transfers between devices, per_device(): lax.all_to_all(jnp.broadcast_to(pair[None], (4,) + pair.shape), PLANE, 0,...  7.74 us
    ppermute x1, starting transfers between devices, per_device(): weight_block = lax.ppermute(kv_weight, ALL, weight_to_plane())  7.35 us
  transfers between devices with their start and end apart: 16, of which 11 were waited for; matrix products, arithmetic and copies ran while one was open for 11% of the time, Pallas kernels for 6%

profile of v1, /device:TPU:14, one launch (start us, length us, event | category | flops | bytes accessed | tf_op | source)
XLA Modules:
  0.0 280.6 jit_solution(9195391381490895468)
XLA Ops:
  7.2 1.1 reshape_squeeze.15
  9.0 2.2 broadcast_in_dim.18
  11.2 7.3 %all-to-all-start = ((bf16[16,40,1176]{2,1,0:T(8,128)(2,1)}), bf16[16,40,1176]{2,1,0:T(8,128)(2,1)}, u32[]{:S(2)}, u32[]{:S(2)}) async-start(bf16[16,40,1176]{2,1,0:T(8,128)(2,1)} %broadcast_in_dim.18), calls=%async_computation | async-start | bytes 3276800 | tf_op jit(solution)/shard_map/all_to_all | solution.py:212
  19.3 7.3 %collective-permute-start = (bf16[256,256]{1,0:T(8,128)(2,1)}, bf16[256,256]{1,0:T(8,128)(2,1)S(1)}, u32[]{:S(2)}, u32[]{:S(2)}) collective-permute-start(bf16[256,256]{1,0:T(8,128)(2,1)} %param.26), channel_id=1, source_target_pairs={{0,0},{1,32},{2,64},{3,96},{4,128},{5,160},{6,192},{7,224},{8,8},{... | collective-permute-start | bytes 393224 | tf_op jit(solution)/shard_map/ppermute | solution.py:224
  26.6 12.2 %collective-permute-done = bf16[256,256]{1,0:T(8,128)(2,1)S(1)} collective-permute-done((bf16[256,256]{1,0:T(8,128)(2,1)}, bf16[256,256]{1,0:T(8,128)(2,1)S(1)}, u32[]{:S(2)}, u32[]{:S(2)}) %collective-permute-start) | collective-permute-done | bytes 131104 | tf_op jit(solution)/shard_map/ppermute | solution.py:224
  38.8 4.8 %all-to-all-done = bf16[16,40,1176]{2,1,0:T(8,128)(2,1)} async-done(((bf16[16,40,1176]{2,1,0:T(8,128)(2,1)}), bf16[16,40,1176]{2,1,0:T(8,128)(2,1)}, u32[]{:S(2)}, u32[]{:S(2)}) %all-to-all-start) | async-done | bytes 1505312 | tf_op jit(solution)/shard_map/all_to_all | solution.py:212
  43.6 0.8 broadcast_in_dim.19
  44.4 12.6 %all-to-all-start.1 = ((bf16[8,128,256]{2,1,0:T(8,128)(2,1)}), bf16[8,128,256]{2,1,0:T(8,128)(2,1)}, u32[]{:S(2)}, u32[]{:S(2)}) async-start(bf16[8,128,256]{2,1,0:T(8,128)(2,1)} %broadcast_in_dim.19), calls=%async_computation.1 | async-start | bytes 1048576 | tf_op jit(solution)/shard_map/all_to_all | solution.py:177
  57.8 16.4 %all-to-all-done.1.left_ref = bf16[8,128,256]{2,1,0:T(8,128)(2,1)} async-done(((bf16[8,128,256]{2,1,0:T(8,128)(2,1)}), bf16[8,128,256]{2,1,0:T(8,128)(2,1)}, u32[]{:S(2)}, u32[]{:S(2)}) %all-to-all-start.1) | async-done | bytes 524320 | tf_op jit(solution)/shard_map/all_to_all | solution.py:177
  74.2 1.3 reverse_select_fusion.2
  75.7 1.3 copy.32
  77.1 2.2 reshape.104
  79.2 2.2 select_bitcast_fusion.1
  81.5 2.0 pad_maximum_fusion
  83.5 5.8 %fusion.35 = f32[512,1280]{1,0:T(8,128)} fusion(bf16[512,1176]{1,0:T(8,128)(2,1)} %all-gather.4.cloned.1.call-done, bf16[1280,1176]{1,0:T(8,128)(2,1)} %bitcast.50), kind=kOutput, calls=%fused_computation.67 | convolution fusion | flops 1541406720 | bytes 6836224 | tf_op jit(solution)/shard_map/dot_general | solution.py:231
  89.3 4.8 %all-to-all-start.2 = ((bf16[4,128,512]{2,1,0:T(8,128)(2,1)}), bf16[4,128,512]{2,1,0:T(8,128)(2,1)}, u32[]{:S(2)}, u32[]{:S(2)}) async-start(bf16[4,128,512]{2,1,0:T(8,128)(2,1)} %reshape.104), calls=%async_computation.2 | async-start | bytes 1048576 | tf_op jit(solution)/shard_map/all_to_all | solution.py:235
  94.1 2.0 reduce_sum.77
  96.1 2.3 multiply_reduce_fusion
  99.2 1.1 fusion.34
  100.2 5.4 %all-to-all-done.2.own_ref = bf16[4,128,512]{2,1,0:T(8,128)(2,1)} async-done(((bf16[4,128,512]{2,1,0:T(8,128)(2,1)}), bf16[4,128,512]{2,1,0:T(8,128)(2,1)}, u32[]{:S(2)}, u32[]{:S(2)}) %all-to-all-start.2) | async-done | bytes 524320 | tf_op jit(solution)/shard_map/all_to_all | solution.py:235
  105.7 2.6 fusion.14
  109.0 5.8 %collective-permute-done.2.left_ref = bf16[112,320]{1,0:T(8,128)(2,1)S(1)} collective-permute-done((bf16[112,320]{1,0:T(8,128)(2,1)S(1)}, bf16[112,320]{1,0:T(8,128)(2,1)S(1)}, u32[]{:S(2)}, u32[]{:S(2)}) %collective-permute-start.2) | collective-permute-done | bytes 71712 | tf_op jit(solution)/shard_map/ppermute | solution.py:33
  115.4 7.3 %shard_map.165 = bf16[8,112,1024]{2,1,0:T(8,128)(2,1)} custom-call(bf16[112,320]{1,0:T(8,128)(2,1)} %copy-done.6, bf16[320,8192]{1,0:T(8,128)(2,1)} %right_ref.1), custom_call_target="tpu_custom_call" | custom-call | flops 587202560 | bytes 5242880 | tf_op jit(solution)/shard_map/pallas_call | solution.py:65
  122.7 4.5 %all-to-all-start.3 = ((bf16[8,112,1024]{2,1,0:T(8,128)(2,1)}), bf16[8,112,1024]{2,1,0:T(8,128)(2,1)}, u32[]{:S(2)}, u32[]{:S(2)}) async-start(bf16[8,112,1024]{2,1,0:T(8,128)(2,1)} %shard_map.165), calls=%async_computation.3 | async-start | bytes 3670016 | tf_op jit(solution)/shard_map/all_to_all | solution.py:177
  129.1 43.8 %all-to-all-done.3 = bf16[8,112,1024]{2,1,0:T(8,128)(2,1)} async-done(((bf16[8,112,1024]{2,1,0:T(8,128)(2,1)}), bf16[8,112,1024]{2,1,0:T(8,128)(2,1)}, u32[]{:S(2)}, u32[]{:S(2)}) %all-to-all-start.3) | async-done | bytes 1835040 | tf_op jit(solution)/shard_map/all_to_all | solution.py:177
  172.9 2.6 convert_reduce_fusion
  175.6 7.0 %shard_map.167 = f32[128,1024]{1,0:T(8,128)} custom-call(bf16[8,128,256]{2,1,0:T(8,128)(2,1)} %all-to-all-done.1.left_ref, bf16[8,1024,256]{2,1,0:T(8,128)(2,1)} %bitcast.47), custom_call_target="tpu_custom_call" | custom-call | flops 536870912 | bytes 4194304 | tf_op jit(solution)/shard_map/pallas_call | solution.py:121
  182.6 2.3 multiply_reduce_fusion.2
  185.0 10.1 %all_to_all.40 = f32[8,2,128]{2,1,0:T(2,128)S(1)} all-to-all(f32[8,2,128]{2,1,0:T(2,128)S(1)} %broadcast_in_dim.23), channel_id=1, replica_groups=mesh['sec'=2,'dp'=16,'tp'=8] {'tp'}, dimensions={0} | all-to-all | bytes 16384 | tf_op jit(solution)/shard_map/all_to_all | solution.py:177
  195.1 2.1 multiply_convert_fusion
  197.4 1.3 collective-permute-done.5
  198.8 1.1 broadcast_in_dim.26
  199.8 4.9 %all-to-all-start.6 = ((bf16[4,2,128,512]{3,2,1,0:T(8,128)(2,1)}), bf16[4,2,128,512]{3,2,1,0:T(8,128)(2,1)}, u32[]{:S(2)}, u32[]{:S(2)}) async-start(bf16[4,2,128,512]{3,2,1,0:T(8,128)(2,1)} %broadcast_in_dim.26), calls=%async_computation.6 | async-start | bytes 2097152 | tf_op jit(solution)/shard_map/all_to_all | solution.py:279
  204.7 6.6 %shard_map.166 = bf16[8,128,256]{2,1,0:T(8,128)(2,1)} custom-call(bf16[128,1024]{1,0:T(8,128)(2,1)} %get-tuple-element.32.left_ref, bf16[8,1024,256]{2,1,0:T(8,128)(2,1)} %bitcast.48), custom_call_target="tpu_custom_call" | custom-call | flops 536870912 | bytes 4194304 | tf_op jit(solution)/shard_map/pallas_call | solution.py:89
  211.3 7.7 %all-to-all-done.6.normed_ref = bf16[4,2,128,512]{3,2,1,0:T(8,128)(2,1)} async-done(((bf16[4,2,128,512]{3,2,1,0:T(8,128)(2,1)}), bf16[4,2,128,512]{3,2,1,0:T(8,128)(2,1)}, u32[]{:S(2)}, u32[]{:S(2)}) %all-to-all-start.6) | async-done | bytes 1048608 | tf_op jit(solution)/shard_map/all_to_all | solution.py:279
  219.0 4.1 %all-to-all-start.4 = ((bf16[8,128,256]{2,1,0:T(8,128)(2,1)}), bf16[8,128,256]{2,1,0:T(8,128)(2,1)}, u32[]{:S(2)}, u32[]{:S(2)}) async-start(bf16[8,128,256]{2,1,0:T(8,128)(2,1)} %shard_map.166), calls=%async_computation.4 | async-start | bytes 1048576 | tf_op jit(solution)/shard_map/all_to_all | solution.py:177
  223.2 3.1 %shard_map.168 = bf16[4,256,256]{2,1,0:T(8,128)(2,1)} custom-call(bf16[4,2,128,512]{3,2,1,0:T(8,128)(2,1)} %all-to-all-done.6.normed_ref, bf16[4,128,512]{2,1,0:T(8,128)(2,1)} %all-to-all-done.2.own_ref, bf16[4,128,512]{2,1,0:T(8,128)(2,1)} %collective-permute-done.3.other_ref), custom_call_target="tpu_custom_call" | custom-call | flops 536870912 | bytes 3145728 | tf_op jit(solution)/shard_map/pallas_call | solution.py:151
  226.3 14.2 %all-to-all-done.4 = bf16[8,128,256]{2,1,0:T(8,128)(2,1)} async-done(((bf16[8,128,256]{2,1,0:T(8,128)(2,1)}), bf16[8,128,256]{2,1,0:T(8,128)(2,1)}, u32[]{:S(2)}, u32[]{:S(2)}) %all-to-all-start.4) | async-done | bytes 524320 | tf_op jit(solution)/shard_map/all_to_all | solution.py:177
  240.4 6.3 %all-to-all-start.7 = ((bf16[4,256,256]{2,1,0:T(8,128)(2,1)}), bf16[4,256,256]{2,1,0:T(8,128)(2,1)}, u32[]{:S(2)}, u32[]{:S(2)}) async-start(bf16[4,256,256]{2,1,0:T(8,128)(2,1)} %shard_map.168), calls=%async_computation.7 | async-start | bytes 1048576 | tf_op jit(solution)/shard_map/all_to_all | solution.py:283
  247.0 1.5 collective-permute-start.4
  248.6 4.9 %collective-permute-done.4 = bf16[112,1024]{1,0:T(8,128)(2,1)S(1)} collective-permute-done((bf16[112,1024]{1,0:T(8,128)(2,1)S(1)}, bf16[112,1024]{1,0:T(8,128)(2,1)S(1)}, u32[]{:S(2)}, u32[]{:S(2)}) %collective-permute-start.4) | collective-permute-done | bytes 229408 | tf_op jit(solution)/shard_map/ppermute | solution.py:33
  254.2 1.1 convert_reduce_fusion.1
  255.4 1.1 reduce_sum.85
  256.5 1.9 collective-permute-start.6
  258.4 0.7 fusion.24
  259.1 12.3 %collective-permute-done.6 = bf16[256,256]{1,0:T(8,128)(2,1)S(1)} collective-permute-done((bf16[256,256]{1,0:T(8,128)(2,1)S(1)}, bf16[256,256]{1,0:T(8,128)(2,1)S(1)}, u32[]{:S(2)}, u32[]{:S(2)}) %collective-permute-start.6) | collective-permute-done | bytes 131104 | tf_op jit(solution)/shard_map/ppermute | solution.py:285
  271.4 0.7 convert_element_type.63
  272.2 1.6 copy.41
  (62 shorter events, 7.4 us)
Async XLA Ops:
  7.2 98.5 %copy-start = (bf16[5120,320]{0,1:T(8,128)(2,1)S(1)}, bf16[5120,320]{0,1:T(8,128)(2,1)}, u32[]{:S(2)}) copy-start(bf16[5120,320]{0,1:T(8,128)(2,1)} %param.20) | copy-start | bytes 9830404
  9.0 34.6 %copy-start.7 = (bf16[1,128,256]{2,1,0:T(8,128)(2,1)S(1)}, bf16[1,128,256]{2,1,0:T(8,128)(2,1)}, u32[]{:S(2)}) copy-start(bf16[1,128,256]{2,1,0:T(8,128)(2,1)} %param.27) | copy-start | bytes 196612
  11.2 32.4 %all-to-all-start = ((bf16[16,40,1176]{2,1,0:T(8,128)(2,1)}), bf16[16,40,1176]{2,1,0:T(8,128)(2,1)}, u32[]{:S(2)}, u32[]{:S(2)}) async-start(bf16[16,40,1176]{2,1,0:T(8,128)(2,1)} %broadcast_in_dim.18), calls=%async_computation | async-start | bytes 3276800 | tf_op jit(solution)/shard_map/all_to_all | solution.py:212
  18.5 65.0 %all-gather.4.cloned.1.call-start = ((), (), s32[]{:S(2)}) async-start(), calls=%async_computation.8 | async-start | bytes 1474560 | tf_op jit(solution)/shard_map/all_gather | solution.py:210
  19.3 19.6 %collective-permute-start = (bf16[256,256]{1,0:T(8,128)(2,1)}, bf16[256,256]{1,0:T(8,128)(2,1)S(1)}, u32[]{:S(2)}, u32[]{:S(2)}) collective-permute-start(bf16[256,256]{1,0:T(8,128)(2,1)} %param.26), channel_id=1, source_target_pairs={{0,0},{1,32},{2,64},{3,96},{4,128},{5,160},{6,192},{7,224},{8,8},{... | collective-permute-start | bytes 393224 | tf_op jit(solution)/shard_map/ppermute | solution.py:224
  38.8 18.4 %copy-start.5 = (bf16[256,256]{1,0:T(8,128)(2,1)}, bf16[256,256]{1,0:T(8,128)(2,1)S(1)}, u32[]{:S(2)}) copy-start(bf16[256,256]{1,0:T(8,128)(2,1)S(1)} %collective-permute-done) | copy-start | bytes 393220
  44.4 29.8 %all-to-all-start.1 = ((bf16[8,128,256]{2,1,0:T(8,128)(2,1)}), bf16[8,128,256]{2,1,0:T(8,128)(2,1)}, u32[]{:S(2)}, u32[]{:S(2)}) async-start(bf16[8,128,256]{2,1,0:T(8,128)(2,1)} %broadcast_in_dim.19), calls=%async_computation.1 | async-start | bytes 1048576 | tf_op jit(solution)/shard_map/all_to_all | solution.py:177
  57.1 118.5 %all-gather.6.cloned.1.call-start = ((), (), s32[]{:S(2)}) async-start(), calls=%async_computation.9 | async-start | bytes 4325376 | tf_op jit(solution)/shard_map/all_gather | solution.py:226
  57.1 22.1 %collective-permute-start.1 = (bf16[16,40,1176]{2,1,0:T(8,128)(2,1)}, bf16[16,40,1176]{2,1,0:T(8,128)(2,1)}, u32[]{:S(2)}, u32[]{:S(2)}) collective-permute-start(bf16[16,40,1176]{2,1,0:T(8,128)(2,1)} %all-to-all-done), channel_id=1, source_target_pairs={{0,8},{8,0},{16,24},{24,16},{32,40},{40,32},{48,56},{56,48},{64,72... | collective-permute-start | bytes 4515848 | tf_op jit(solution)/shard_map/ppermute | solution.py:29
  89.3 16.4 %all-to-all-start.2 = ((bf16[4,128,512]{2,1,0:T(8,128)(2,1)}), bf16[4,128,512]{2,1,0:T(8,128)(2,1)}, u32[]{:S(2)}, u32[]{:S(2)}) async-start(bf16[4,128,512]{2,1,0:T(8,128)(2,1)} %reshape.104), calls=%async_computation.2 | async-start | bytes 1048576 | tf_op jit(solution)/shard_map/all_to_all | solution.py:235
  94.1 4.3 %copy-start.9 = (f32[1280]{0:T(1024)S(1)}, f32[1280]{0:T(1024)}, u32[]{:S(2)}) copy-start(f32[1280]{0:T(1024)} %param.19) | copy-start | bytes 15364
  94.1 4.3 %copy-start.10 = (f32[1280]{0:T(1024)S(1)}, f32[1280]{0:T(1024)}, u32[]{:S(2)}) copy-start(f32[1280]{0:T(1024)} %param.18) | copy-start | bytes 15364
  96.1 2.6 copy-start.1
  98.7 7.0 %copy-start.13 = (f32[320]{0:T(512)S(1)}, f32[320]{0:T(512)}, u32[]{:S(2)}) copy-start(f32[320]{0:T(512)} %param.21) | copy-start | bytes 3844
  105.7 9.1 %collective-permute-start.3 = (bf16[4,128,512]{2,1,0:T(8,128)(2,1)}, bf16[4,128,512]{2,1,0:T(8,128)(2,1)}, u32[]{:S(2)}, u32[]{:S(2)}) collective-permute-start(bf16[4,128,512]{2,1,0:T(8,128)(2,1)} %all-to-all-done.2.own_ref), channel_id=1, source_target_pairs={{0,8},{8,0},{16,24},{24,16},{32,40},{40,32},{48,56},{56,48},{64,72... | collective-permute-start | bytes 1572872 | tf_op jit(solution)/shard_map/ppermute | solution.py:29
  108.5 6.3 %collective-permute-start.2 = (bf16[112,320]{1,0:T(8,128)(2,1)S(1)}, bf16[112,320]{1,0:T(8,128)(2,1)S(1)}, u32[]{:S(2)}, u32[]{:S(2)}) collective-permute-start(bf16[112,320]{1,0:T(8,128)(2,1)S(1)} %reshape.108), channel_id=1, source_target_pairs={{0,128},{128,0},{1,129},{129,1},{2,130},{130,2},{3,131},{131,3},{4... | collective-permute-start | bytes 215048 | tf_op jit(solution)/shard_map/ppermute | solution.py:33
  114.8 0.6 copy-start.6
  122.7 4.5 %copy-start.14 = (s32[32]{0:T(128)S(1)}, s32[32]{0:T(128)}, u32[]{:S(2)}) copy-start(s32[32]{0:T(128)} %param.15) | copy-start | bytes 388
  122.7 5.7 %copy-start.12 = (s32[1,112]{1,0:T(1,128)S(1)}, s32[1,112]{1,0:T(1,128)}, u32[]{:S(2)}) copy-start(s32[1,112]{1,0:T(1,128)} %param.16) | copy-start | bytes 1348
  122.7 50.2 %all-to-all-start.3 = ((bf16[8,112,1024]{2,1,0:T(8,128)(2,1)}), bf16[8,112,1024]{2,1,0:T(8,128)(2,1)}, u32[]{:S(2)}, u32[]{:S(2)}) async-start(bf16[8,112,1024]{2,1,0:T(8,128)(2,1)} %shard_map.165), calls=%async_computation.3 | async-start | bytes 3670016 | tf_op jit(solution)/shard_map/all_to_all | solution.py:177
  175.6 7.1 %copy-start.3 = (bf16[1,128,1024]{2,1,0:T(8,128)(2,1)S(1)}, bf16[1,128,1024]{2,1,0:T(8,128)(2,1)}, u32[]{:S(2)}) copy-start(bf16[1,128,1024]{2,1,0:T(8,128)(2,1)} %param.24) | copy-start | bytes 786436
  175.6 7.1 %copy-start.8 = (f32[1024]{0:T(1024)S(1)}, f32[1024]{0:T(1024)}, u32[]{:S(2)}) copy-start(f32[1024]{0:T(1024)} %param.25) | copy-start | bytes 12292
  175.6 7.1 %copy-start.11 = (f32[1024]{0:T(1024)S(1)}, f32[1024]{0:T(1024)}, u32[]{:S(2)}) copy-start(f32[1024]{0:T(1024)} %param.23) | copy-start | bytes 12292
  197.3 49.5 %copy-start.2 = (bf16[128,1024]{1,0:T(8,128)(2,1)}, bf16[128,1024]{1,0:T(8,128)(2,1)S(1)}, u32[]{:S(2)}) copy-start(bf16[128,1024]{1,0:T(8,128)(2,1)S(1)} %get-tuple-element.31) | copy-start | bytes 786436
  197.3 1.4 collective-permute-start.5
  199.8 19.2 %all-to-all-start.6 = ((bf16[4,2,128,512]{3,2,1,0:T(8,128)(2,1)}), bf16[4,2,128,512]{3,2,1,0:T(8,128)(2,1)}, u32[]{:S(2)}, u32[]{:S(2)}) async-start(bf16[4,2,128,512]{3,2,1,0:T(8,128)(2,1)} %broadcast_in_dim.26), calls=%async_computation.6 | async-start | bytes 2097152 | tf_op jit(solution)/shard_map/all_to_all | solution.py:279
  219.0 21.4 %all-to-all-start.4 = ((bf16[8,128,256]{2,1,0:T(8,128)(2,1)}), bf16[8,128,256]{2,1,0:T(8,128)(2,1)}, u32[]{:S(2)}, u32[]{:S(2)}) async-start(bf16[8,128,256]{2,1,0:T(8,128)(2,1)} %shard_map.166), calls=%async_computation.4 | async-start | bytes 1048576 | tf_op jit(solution)/shard_map/all_to_all | solution.py:177
  240.4 14.9 %all-to-all-start.7 = ((bf16[4,256,256]{2,1,0:T(8,128)(2,1)}), bf16[4,256,256]{2,1,0:T(8,128)(2,1)}, u32[]{:S(2)}, u32[]{:S(2)}) async-start(bf16[4,256,256]{2,1,0:T(8,128)(2,1)} %shard_map.168), calls=%async_computation.7 | async-start | bytes 1048576 | tf_op jit(solution)/shard_map/all_to_all | solution.py:283
  247.0 6.5 %collective-permute-start.4 = (bf16[112,1024]{1,0:T(8,128)(2,1)S(1)}, bf16[112,1024]{1,0:T(8,128)(2,1)S(1)}, u32[]{:S(2)}, u32[]{:S(2)}) collective-permute-start(bf16[112,1024]{1,0:T(8,128)(2,1)S(1)} %convolution_convert_fusion), channel_id=1, source_target_pairs={{0,128},{128,0},{1,129},{129,1},{2,130},{130,2},{3,131},{131,3},{4... | collective-permute-start | bytes 688136 | tf_op jit(solution)/shard_map/ppermute | solution.py:33
  253.5 0.7 copy-start.4
  256.5 14.9 %collective-permute-start.6 = (bf16[256,256]{1,0:T(8,128)(2,1)S(1)}, bf16[256,256]{1,0:T(8,128)(2,1)S(1)}, u32[]{:S(2)}, u32[]{:S(2)}) collective-permute-start(bf16[256,256]{1,0:T(8,128)(2,1)S(1)} %reduce_sum.85), channel_id=1, source_target_pairs={{0,0},{1,33},{2,66},{3,99},{4,132},{5,165},{6,198},{7,231},{8,16},... | collective-permute-start | bytes 393224 | tf_op jit(solution)/shard_map/ppermute | solution.py:285
Sparse Core Ops, SparseCore 0:
  21.7 44.1 all-gather.3
  68.4 63.1 all-gather.5

commit v2 on v1

--- a/solution.py
+++ b/solution.py
@@ -2,6 +2,7 @@
 import jax.numpy as jnp
 from jax import lax
 from jax.experimental import pallas as pl
+from jax.experimental.pallas import tpu as pltpu
 from jax.sharding import PartitionSpec as P
 
 WIDTH = 8192
@@ -53,84 +54,111 @@
     return route
 
 
-def column_product_kernel(left_ref, right_ref, out_ref):
-    out_ref[0] = jnp.dot(
-        left_ref[...], right_ref[...], preferred_element_type=F32
-    ).astype(out_ref.dtype)
-
-
-def column_product(left, right):
-    rows, depth = left.shape
-    width = right.shape[1] // N_TP
-    return pl.pallas_call(
-        column_product_kernel,
-        grid=(N_TP,),
+def share_kernel(place_ref, block_ref, out_ref):
+    out_ref[0] = block_ref[...]
+
+
+def take_share(weight, place):
+    return pl.pallas_call(
+        share_kernel,
+        grid_spec=pltpu.PrefetchScalarGridSpec(
+            num_scalar_prefetch=1,
+            grid=(N_TP,),
+            in_specs=[
+                pl.BlockSpec((40, 256), lambda i, place: (place[0] // 4, 4 * i + place[0] % 4))
+            ],
+            out_specs=pl.BlockSpec((1, 40, 256), lambda i, place: (i, 0, 0)),
+        ),
+        out_shape=jax.ShapeDtypeStruct((N_TP, 40, 256), BF),
+        cost_estimate=pl.CostEstimate(flops=0, bytes_accessed=640 * 512, transcendentals=0),
+    )(place.astype(jnp.int32)[None], weight)
+
+
+def vision_kernel(left_ref, right_ref, bias_ref, out_ref):
+    right = right_ref[:, 0].reshape(left_ref.shape[1], -1)
+    total = jnp.dot(left_ref[...], right, preferred_element_type=F32) + bias_ref[...]
+    out_ref[...] = total.astype(BF)
+
+
+def vision_product(hidden, gathered, bias):
+    rows, depth = hidden.shape
+    return pl.pallas_call(
+        vision_kernel,
+        grid=(4,),
         in_specs=[
             pl.BlockSpec((rows, depth), lambda i: (0, 0)),
-            pl.BlockSpec((depth, width), lambda i: (0, i)),
+            pl.BlockSpec((8, 1, 320, 256), lambda i: (0, i, 1, 0)),
+            pl.BlockSpec((1, 256), lambda i: (0, i)),
         ],
-        out_specs=pl.BlockSpec((1, rows, width), lambda i: (i, 0, 0)),
-        out_shape=jax.ShapeDtypeStruct((N_TP, rows, width), BF),
+        out_specs=pl.BlockSpec((rows, 256), lambda i: (0, i)),
+        out_shape=jax.ShapeDtypeStruct((rows, 1024), BF),
         cost_estimate=pl.CostEstimate(
-            flops=2 * rows * right.size, bytes_accessed=2 * right.size, transcendentals=0
-        ),
-    )(left, right)
+            flops=2 * rows * depth * 1024, bytes_accessed=2 * depth * 1024, transcendentals=0
+        ),
+    )(hidden, gathered, bias[None])
 
 
 def block_product_kernel(left_ref, right_ref, out_ref):
     out_ref[0] = jnp.dot(
-        left_ref[...], right_ref[0], preferred_element_type=F32
+        left_ref[...], right_ref[0].reshape(1024, 256), preferred_element_type=F32
     ).astype(out_ref.dtype)
 
 
-def block_product(left, right):
-    rows, depth = left.shape
-    width = right.shape[2]
+def block_product(left, gathered):
+    rows = left.shape[0]
     return pl.pallas_call(
         block_product_kernel,
         grid=(N_TP,),
         in_specs=[
-            pl.BlockSpec((rows, depth), lambda i: (0, 0)),
-            pl.BlockSpec((1, depth, width), lambda i: (i, 0, 0)),
+            pl.BlockSpec((rows, 1024), lambda i: (0, 0)),
+            pl.BlockSpec((1, 4, 256, 256), lambda i: (i, 0, 0, 0)),
         ],
-        out_specs=pl.BlockSpec((1, rows, width), lambda i: (i, 0, 0)),
-        out_shape=jax.ShapeDtypeStruct((N_TP, rows, width), BF),
+        out_specs=pl.BlockSpec((1, rows, 256), lambda i: (i, 0, 0)),
+        out_shape=jax.ShapeDtypeStruct((N_TP, rows, 256), BF),
         cost_estimate=pl.CostEstimate(
-            flops=2 * rows * right.size, bytes_accessed=2 * right.size, transcendentals=0
-        ),
-    )(left, right)
-
-
-def block_sum_kernel(left_ref, right_ref, out_ref):
+            flops=2 * rows * 1024 * 2048, bytes_accessed=4 << 20, transcendentals=0
+        ),
+    )(left, gathered)
+
+
+def block_sum_kernel(left_ref, right_ref, out_ref, total_ref):
+    step = pl.program_id(0)
     part = lax.dot_general(
-        left_ref[0], right_ref[0], (((1,), (1,)), ((), ())), preferred_element_type=F32
-    )
-
-    @pl.when(pl.program_id(0) == 0)
+        right_ref[0].reshape(1024, 256),
+        left_ref[0],
+        (((1,), (1,)), ((), ())),
+        preferred_element_type=F32,
+    )
+
+    @pl.when(step == 0)
     def _():
-        out_ref[...] = part
-
-    @pl.when(pl.program_id(0) > 0)
+        total_ref[...] = part
+
+    @pl.when(step > 0)
     def _():
-        out_ref[...] += part
-
-
-def block_sum(left, right):
-    rows, width = left.shape[1:]
-    depth = right.shape[1]
+        total_ref[...] += part
+
+    @pl.when(step == N_TP - 1)
+    def _():
+        out_ref[...] = total_ref[...].T
+
+
+def block_sum(left, gathered):
+    rows = left.shape[1]
     return pl.pallas_call(
         block_sum_kernel,
         grid=(N_TP,),
         in_specs=[
-            pl.BlockSpec((1, rows, width), lambda i: (i, 0, 0)),
-            pl.BlockSpec((1, depth, width), lambda i: (i, 0, 0)),
+            pl.BlockSpec((1, rows, 256), lambda i: (i, 0, 0)),
+            pl.BlockSpec((1, 4, 256, 256), lambda i: (i, 0, 0, 0)),
         ],
-        out_specs=pl.BlockSpec((rows, depth), lambda i: (0, 0)),
-        out_shape=jax.ShapeDtypeStruct((rows, depth), F32),
+        out_specs=pl.BlockSpec((rows, 1024), lambda i: (0, 0)),
+        out_shape=jax.ShapeDtypeStruct((rows, 1024), F32),
+        scratch_shapes=[pltpu.VMEM((1024, rows), F32)],
         cost_estimate=pl.CostEstimate(
-            flops=2 * rows * right.size, bytes_accessed=2 * right.size, transcendentals=0
-        ),
-    )(left, right)
+            flops=2 * rows * 1024 * 2048, bytes_accessed=4 << 20, transcendentals=0
+        ),
+    )(left, gathered)
 
 
 def line_product_kernel(normed_ref, own_ref, other_ref, out_ref):
@@ -206,9 +234,9 @@
     tokens = patches.shape[1] // MERGE_PATCHES
     rows = patches[0].reshape(tokens, MERGE_PATCHES, -1).transpose(1, 0, 2)
     rows = jnp.pad(rows, ((0, 0), (0, 16 - tokens), (0, 0))).reshape(MERGE_PATCHES * 16, -1)
-    columns, rows = lax.optimization_barrier((pe_weight.T, rows))
     patch_all = lax.all_gather(rows, "tp", tiled=True)
 
+    columns = pe_weight.T
     mine = lax.all_to_all(
         jnp.broadcast_to(columns[None], (16,) + columns.shape),
         PLANE,
@@ -216,25 +244,25 @@
         0,
         axis_index_groups=SAME_CORE,
     )
+    place = sec * 16 + dp
+    weight_block = lax.ppermute(kv_weight, ALL, weight_to_plane())
+    share, weight_block, mine = lax.optimization_barrier(
+        (take_share(w_out, place), weight_block, mine)
+    )
+    share = exchange_tp(share).reshape(320, 256)
+
+    shard = jnp.concatenate([weight_block, jnp.zeros((64, 256), BF), share], axis=0)
+    gathered = lax.all_gather(shard, PLANE).reshape(8, 4, 640, 256)
+
+    cot_input, _ = lax.optimization_barrier((kv_cotangent[0], share))
+    cotangents = gather_tp(cot_input)
     other = swap_cores(mine)
     first = jnp.where(core == 0, mine, other)
     second = jnp.where(core == 0, other, mine)
     full_patch = jnp.stack([first, second], axis=1).reshape(1280, -1)
-
-    weight_block = lax.ppermute(kv_weight, ALL, weight_to_plane())
-    weight_block, cot_input, _ = lax.optimization_barrier((weight_block, kv_cotangent[0], mine))
-    weight_all = lax.all_gather(weight_block, PLANE).reshape(N_TP, 1024, 256)
-
-    cotangents = gather_tp(cot_input)
-    cot_line = flip_bits(cotangents, tp)
-    cot_line = cot_line.reshape(4, 2, 128, 256).transpose(0, 2, 1, 3).reshape(4, 128, 512)
     projected = lax.dot_general(
         patch_all, full_patch, (((1,), (1,)), ((), ())), preferred_element_type=F32
     )
-    cot_line, projected = lax.optimization_barrier((cot_line, projected))
-    cot_line = lax.all_to_all(cot_line, PLANE, 0, 0, axis_index_groups=SAME_X)
-    cot_other = swap_cores(cot_line)
-
     embedded = layer_norm(projected, ln_gain, ln_bias).astype(BF)
     embedded = embedded.reshape(N_TP, MERGE_PATCHES, 16, 1280)
     merged = jnp.concatenate(
@@ -243,10 +271,18 @@
     before_gelu = jnp.dot(merged, w_in, preferred_element_type=F32) + b_in
     hidden = jax.nn.gelu(before_gelu, approximate=False).astype(BF)
     hidden = hidden.reshape(N_TP, 16, -1)[:, :tokens].reshape(N_TP * tokens, -1)
-    hidden = swap_halves(hidden)
-    hidden, cot_line, cot_other = lax.optimization_barrier((hidden, cot_line, cot_other))
-    partial = column_product(hidden, w_out)
-    vision = (jnp.sum(exchange_tp(partial).astype(F32), axis=0) + b_out).astype(BF)
+    hidden = swap_halves(hidden).T
+    hidden, cotangents = lax.optimization_barrier((hidden, cotangents))
+    hidden = gather_tp(hidden)
+
+    cot_line = flip_bits(cotangents, tp)
+    cot_line = cot_line.reshape(4, 2, 128, 256).transpose(0, 2, 1, 3).reshape(4, 128, 512)
+    cot_line, hidden = lax.optimization_barrier((cot_line, hidden))
+    cot_line = lax.all_to_all(cot_line, PLANE, 0, 0, axis_index_groups=SAME_X)
+    cot_other = swap_cores(cot_line)
+
+    hidden = hidden.reshape(N_TP, 8, 40, -1).transpose(1, 0, 2, 3).reshape(2560, -1).T
+    vision = vision_product(hidden, gathered, b_out)
 
     line_index = jnp.arange(128)
     slot_positions = positions[0]
@@ -257,9 +293,10 @@
     image_rows = jnp.any(selector, axis=1, keepdims=True)
     combined = jnp.where(image_rows, placed, text_embeds[0].astype(F32))
 
-    normed_grad = block_sum(cotangents, weight_all)
+    normed_grad = block_sum(cotangents, gathered)
     scaled = normed_grad * rms_gain
     stats = jnp.stack([jnp.sum(combined * combined, axis=1), jnp.sum(scaled * combined, axis=1)])
+    stats, cot_line, cot_other = lax.optimization_barrier((stats, cot_line, cot_other))
     stats = jnp.sum(gather_tp(stats), axis=0)
     row_scale = lax.rsqrt(stats[0] / WIDTH + 1e-06)[:, None]
     row_dot = stats[1][:, None]
@@ -281,10 +318,10 @@
     )
     block = line_product(normed_line, cot_line, cot_other)
     block = lax.all_to_all(block, PLANE, 0, 0, axis_index_groups=SAME_Y)
+    product = block_product(gained.astype(BF), gathered)
     block = jnp.sum(block.astype(F32), axis=0).astype(BF)
+    product, block = lax.optimization_barrier((product, block))
     kv_weight_grad = lax.ppermute(block, ALL, grad_from_plane()).astype(F32)
-
-    product = block_product(gained.astype(BF), weight_all)
     keys_values = jnp.sum(exchange_tp(product).astype(F32), axis=0)
     keys_values = (keys_values * row_scale).astype(BF)
     return (keys_values[None], seq_grad[None], vision_grad[None], kv_weight_grad)

time: 283 us -> 250 us (0.88)
  waiting for transfers between devices: 130 us -> 71.1 us
  blocking collectives: 10.1 us -> 30.6 us
  starting transfers between devices: 56.2 us -> 63.7 us
  other arithmetic: 20.4 us -> 15.9 us
    all_to_all x3 -> x4, waiting for transfers between devices: 74.4 us -> 28.4 us  [exchange_tp(): return lax.all_to_all(blocks, 'tp', 0, 0)]
    all_to_all x0 -> x1, blocking collectives: none -> 18.2 us  [per_device(): lax.all_to_all(jnp.broadcast_to(pair[None], (4,) + pair.shape), PLANE, 0,...]
    ppermute x2, waiting for transfers between devices: 10.7 us -> 1.34 us  [swap_halves(): return lax.ppermute(block, 'sec', [(0, 1), (1, 0)])]
    all_to_all x1 -> x0, waiting for transfers between devices: 7.74 us -> none  [per_device(): lax.all_to_all(jnp.broadcast_to(pair[None], (4,) + pair.shape), PLANE, 0,...]
    all_to_all x3 -> x4, starting transfers between devices: 21.3 us -> 27.9 us  [exchange_tp(): return lax.all_to_all(blocks, 'tp', 0, 0)]
    all_to_all x1, waiting for transfers between devices: 5.44 us -> 11.1 us  [per_device(): cot_line = lax.all_to_all(cot_line, PLANE, 0, 0, axis_index_groups=SAME_X)]
    all_to_all x1 -> x0, starting transfers between devices: 4.86 us -> none  [per_device(): lax.all_to_all(jnp.broadcast_to(pair[None], (4,) + pair.shape), PLANE, 0,...]
    reduce_sum x2 -> x0, other arithmetic: 4.6 us -> none  [the longest x1 2.63 us: per_device(): jnp.sum(exchange_tp(partial).astype(F32), axis=0) + b_out]
  transfers between devices with their start and end apart: 16 -> 16, of which waited for: 11 -> 11; matrix products, arithmetic and copies ran while one was open for 11% -> 13% of each run, Pallas kernels for 6% -> 9%
where the time goes in v2:
time: 250 us; the launch traced here: 245 us
  waiting for transfers between devices  71.1 us (28%)
  starting transfers between devices  63.7 us (25%)
  blocking collectives  30.6 us (12%)
  Pallas kernels  25.9 us (10%)
  other arithmetic  15.9 us (6%)
  local copies, waits for them, and re-layouts  15.6 us (6%)
  between operations  14.4 us (6%)
  matrix products  8.25 us (3%)
    all_to_all x4, waiting for transfers between devices, exchange_tp(): return lax.all_to_all(blocks, 'tp', 0, 0)  28.4 us
    all_to_all x4, starting transfers between devices, exchange_tp(): return lax.all_to_all(blocks, 'tp', 0, 0)  27.9 us
    all_to_all x1, blocking collectives, per_device(): lax.all_to_all(jnp.broadcast_to(pair[None], (4,) + pair.shape), PLANE, 0,...  18.2 us
    ppermute x1, waiting for transfers between devices, per_device(): kv_weight_grad = lax.ppermute(block, ALL, grad_from_plane()).astype(F32)  14.8 us
    all_to_all x1, blocking collectives, exchange_tp(): return lax.all_to_all(blocks, 'tp', 0, 0)  12.5 us
    all_to_all x1, waiting for transfers between devices, per_device(): cot_line = lax.all_to_all(cot_line, PLANE, 0, 0, axis_index_groups=SAME_X)  11.1 us
    ppermute x1, waiting for transfers between devices, per_device(): weight_block = lax.ppermute(kv_weight, ALL, weight_to_plane())  10.7 us
    ppermute x1, starting transfers between devices, per_device(): weight_block = lax.ppermute(kv_weight, ALL, weight_to_plane())  7.34 us
  transfers between devices with their start and end apart: 16, of which 11 were waited for; matrix products, arithmetic and copies ran while one was open for 13% of the time, Pallas kernels for 9%

profile of v2, /device:TPU:14, one launch (start us, length us, event | category | flops | bytes accessed | tf_op | source)
XLA Modules:
  0.0 245.4 jit_solution(6346627022614729120)
XLA Ops:
  7.2 1.1 reshape_squeeze.15
  8.4 0.7 pad.4.clone
  9.1 2.2 broadcast_in_dim.30
  11.3 7.3 %all-to-all-start = ((bf16[16,40,1176]{2,1,0:T(8,128)(2,1)}), bf16[16,40,1176]{2,1,0:T(8,128)(2,1)}, u32[]{:S(2)}, u32[]{:S(2)}) async-start(bf16[16,40,1176]{2,1,0:T(8,128)(2,1)} %broadcast_in_dim.30), calls=%async_computation | async-start | bytes 3276800 | tf_op jit(solution)/shard_map/all_to_all | solution.py:240
  18.6 7.3 %collective-permute-start = (bf16[256,256]{1,0:T(8,128)(2,1)}, bf16[256,256]{1,0:T(8,128)(2,1)S(1)}, u32[]{:S(2)}, u32[]{:S(2)}) collective-permute-start(bf16[256,256]{1,0:T(8,128)(2,1)} %param.26), channel_id=1, source_target_pairs={{0,0},{1,32},{2,64},{3,96},{4,128},{5,160},{6,192},{7,224},{8,8},{... | collective-permute-start | bytes 393224 | tf_op jit(solution)/shard_map/ppermute | solution.py:248
  25.9 4.2 %shard_map.165 = bf16[8,40,256]{2,1,0:T(8,128)(2,1)} custom-call(s32[1]{0:T(128)} %bitcast.4.place_ref, bf16[320,8192]{1,0:T(8,128)(2,1)} %block_ref.1), custom_call_target="tpu_custom_call" | custom-call | bytes 327680 | tf_op jit(solution)/shard_map/pallas_call | solution.py:62
  30.1 10.7 %collective-permute-done = bf16[256,256]{1,0:T(8,128)(2,1)S(1)} collective-permute-done((bf16[256,256]{1,0:T(8,128)(2,1)}, bf16[256,256]{1,0:T(8,128)(2,1)S(1)}, u32[]{:S(2)}, u32[]{:S(2)}) %collective-permute-start) | collective-permute-done | bytes 131104 | tf_op jit(solution)/shard_map/ppermute | solution.py:248
  40.8 2.8 %all-to-all-done = bf16[16,40,1176]{2,1,0:T(8,128)(2,1)} async-done(((bf16[16,40,1176]{2,1,0:T(8,128)(2,1)}), bf16[16,40,1176]{2,1,0:T(8,128)(2,1)}, u32[]{:S(2)}, u32[]{:S(2)}) %all-to-all-start) | async-done | bytes 1505312 | tf_op jit(solution)/shard_map/all_to_all | solution.py:240
  43.6 12.6 %all-to-all-start.1 = ((bf16[8,40,256]{2,1,0:T(8,128)(2,1)}), bf16[8,40,256]{2,1,0:T(8,128)(2,1)S(1)}, u32[]{:S(2)}, u32[]{:S(2)}) async-start(bf16[8,40,256]{2,1,0:T(8,128)(2,1)} %shard_map.165), calls=%async_computation.1 | async-start | bytes 327680 | tf_op jit(solution)/shard_map/all_to_all | solution.py:205
  56.3 9.4 %all-to-all-done.1 = bf16[8,40,256]{2,1,0:T(8,128)(2,1)S(1)} async-done(((bf16[8,40,256]{2,1,0:T(8,128)(2,1)}), bf16[8,40,256]{2,1,0:T(8,128)(2,1)S(1)}, u32[]{:S(2)}, u32[]{:S(2)}) %all-to-all-start.1) | async-done | bytes 163872 | tf_op jit(solution)/shard_map/all_to_all | solution.py:205
  65.7 1.8 pad_maximum_fusion.1
  67.7 0.9 broadcast_in_dim.31
  68.5 4.1 %all-to-all-start.2 = ((bf16[8,128,256]{2,1,0:T(8,128)(2,1)}), bf16[8,128,256]{2,1,0:T(8,128)(2,1)}, u32[]{:S(2)}, u32[]{:S(2)}) async-start(bf16[8,128,256]{2,1,0:T(8,128)(2,1)} %broadcast_in_dim.31), calls=%async_computation.2 | async-start | bytes 1048576 | tf_op jit(solution)/shard_map/all_to_all | solution.py:205
  72.7 2.1 select_bitcast_fusion.1
  74.8 2.1 pad_maximum_fusion
  76.9 4.3 %fusion.34 = (f32[512]{0:T(512)S(1)}, f32[512,1280]{1,0:T(8,128)S(1)}) fusion(bf16[512,1176]{1,0:T(8,128)(2,1)} %all-gather.4.cloned.1.call-done, bf16[1280,1176]{1,0:T(8,128)(2,1)} %bitcast.61), kind=kOutput, calls=%fused_computation.65 | convolution fusion | flops 1542061568 | bytes 6838272 | tf_op jit(solution)/shard_map/dot_general | solution.py:263
  82.7 1.3 fusion.13
  84.2 3.0 %collective-permute-start.2 = (bf16[112,320]{1,0:T(8,128)(2,1)S(1)}, bf16[112,320]{1,0:T(8,128)(2,1)S(1)}, u32[]{:S(2)}, u32[]{:S(2)}) collective-permute-start(bf16[112,320]{1,0:T(8,128)(2,1)S(1)} %reshape.115), channel_id=1, source_target_pairs={{0,128},{128,0},{1,129},{129,1},{2,130},{130,2},{3,131},{131,3},{4... | collective-permute-start | bytes 215048 | tf_op jit(solution)/shard_map/ppermute | solution.py:34
  87.2 3.9 %all-to-all-done.2.left_ref = bf16[8,128,256]{2,1,0:T(8,128)(2,1)} async-done(((bf16[8,128,256]{2,1,0:T(8,128)(2,1)}), bf16[8,128,256]{2,1,0:T(8,128)(2,1)}, u32[]{:S(2)}, u32[]{:S(2)}) %all-to-all-start.2) | async-done | bytes 524320 | tf_op jit(solution)/shard_map/all_to_all | solution.py:205
  91.1 0.9 collective-permute-done.2
  92.2 0.9 broadcast_in_dim.32
  93.1 7.0 %all-to-all-start.3 = ((bf16[8,320,112]{2,1,0:T(8,128)(2,1)}), bf16[8,320,112]{2,1,0:T(8,128)(2,1)}, u32[]{:S(2)}, u32[]{:S(2)}) async-start(bf16[8,320,112]{2,1,0:T(8,128)(2,1)} %broadcast_in_dim.32), calls=%async_computation.3 | async-start | bytes 1310720 | tf_op jit(solution)/shard_map/all_to_all | solution.py:205
  100.1 1.4 reverse_select_fusion.2
  101.7 1.3 copy.42
  103.0 2.2 reshape.118
  105.2 15.1 %all-to-all-done.3 = bf16[8,320,112]{2,1,0:T(8,128)(2,1)} async-done(((bf16[8,320,112]{2,1,0:T(8,128)(2,1)}), bf16[8,320,112]{2,1,0:T(8,128)(2,1)}, u32[]{:S(2)}, u32[]{:S(2)}) %all-to-all-start.3) | async-done | bytes 573472 | tf_op jit(solution)/shard_map/all_to_all | solution.py:205
  120.3 6.1 %all-to-all-start.4 = ((bf16[4,128,512]{2,1,0:T(8,128)(2,1)}), bf16[4,128,512]{2,1,0:T(8,128)(2,1)}, u32[]{:S(2)}, u32[]{:S(2)}) async-start(bf16[4,128,512]{2,1,0:T(8,128)(2,1)} %reshape.118), calls=%async_computation.4 | async-start | bytes 1048576 | tf_op jit(solution)/shard_map/all_to_all | solution.py:281
  127.6 11.1 %all-to-all-done.4.own_ref = bf16[4,128,512]{2,1,0:T(8,128)(2,1)} async-done(((bf16[4,128,512]{2,1,0:T(8,128)(2,1)}), bf16[4,128,512]{2,1,0:T(8,128)(2,1)}, u32[]{:S(2)}, u32[]{:S(2)}) %all-to-all-start.4) | async-done | bytes 524320 | tf_op jit(solution)/shard_map/all_to_all | solution.py:281
  138.9 2.0 copy.44
  140.9 2.1 copy.45
  143.0 7.2 %shard_map.168 = f32[128,1024]{1,0:T(8,128)} custom-call(bf16[8,128,256]{2,1,0:T(8,128)(2,1)} %all-to-all-done.2.left_ref, bf16[8,4,640,256]{3,2,1,0:T(8,128)(2,1)} %bitcast.57), custom_call_target="tpu_custom_call" | custom-call | flops 536870912 | bytes 4194304 | tf_op jit(solution)/shard_map/pallas_call | solution.py:148
  150.2 4.9 %shard_map.166 = bf16[112,1024]{1,0:T(8,128)(2,1)} custom-call(bf16[112,2560]{1,0:T(8,128)(2,1)} %bitcast.63, bf16[8,4,640,256]{3,2,1,0:T(8,128)(2,1)} %bitcast.58, f32[1,1024]{1,0:T(1,128)} %bitcast.79), custom_call_target="tpu_custom_call" | custom-call | flops 587202560 | bytes 5242880 | tf_op jit(solution)/shard_map/pallas_call | solution.py:85
  155.1 2.3 multiply_reduce_fusion.2
  157.4 12.5 %all_to_all.45 = f32[8,2,128]{2,1,0:T(2,128)S(1)} all-to-all(f32[8,2,128]{2,1,0:T(2,128)S(1)} %broadcast_in_dim.35), channel_id=1, replica_groups=mesh['sec'=2,'dp'=16,'tp'=8] {'tp'}, dimensions={0} | all-to-all | bytes 16384 | tf_op jit(solution)/shard_map/all_to_all | solution.py:205
  169.9 2.1 subtract_convert_fusion
  172.2 1.3 collective-permute-done.4
  173.7 18.2 %all_to_all.46.normed_ref = bf16[4,2,128,512]{3,2,1,0:T(8,128)(2,1)} all-to-all(bf16[4,2,128,512]{3,2,1,0:T(8,128)(2,1)S(1)} %broadcast_in_dim.36), channel_id=1, replica_groups={{0,128,16,144},{8,136,24,152},{32,160,48,176},{40,168,56,184},{64,192,8..., dimensions={0} | all-to-all | bytes 2097152 | tf_op jit(solution)/shard_map/all_to_all | solution.py:316
  191.8 3.1 %shard_map.169 = bf16[4,256,256]{2,1,0:T(8,128)(2,1)} custom-call(bf16[4,2,128,512]{3,2,1,0:T(8,128)(2,1)} %all_to_all.46.normed_ref, bf16[4,128,512]{2,1,0:T(8,128)(2,1)} %all-to-all-done.4.own_ref, bf16[4,128,512]{2,1,0:T(8,128)(2,1)} %collective-permute-done.3.other_ref), custom_call_target="tpu_custom_call" | custom-call | flops 536870912 | bytes 3145728 | tf_op jit(solution)/shard_map/pallas_call | solution.py:179
  194.9 6.1 %all-to-all-start.7 = ((bf16[4,256,256]{2,1,0:T(8,128)(2,1)}), bf16[4,256,256]{2,1,0:T(8,128)(2,1)}, u32[]{:S(2)}, u32[]{:S(2)}) async-start(bf16[4,256,256]{2,1,0:T(8,128)(2,1)} %shard_map.169), calls=%async_computation.7 | async-start | bytes 1048576 | tf_op jit(solution)/shard_map/all_to_all | solution.py:320
  201.0 6.6 %shard_map.167 = bf16[8,128,256]{2,1,0:T(8,128)(2,1)} custom-call(bf16[128,1024]{1,0:T(8,128)(2,1)} %get-tuple-element.40.left_ref, bf16[8,4,640,256]{3,2,1,0:T(8,128)(2,1)} %bitcast.59), custom_call_target="tpu_custom_call" | custom-call | flops 536870912 | bytes 4194304 | tf_op jit(solution)/shard_map/pallas_call | solution.py:109
  208.1 1.8 reduce_sum.73
  209.9 4.1 %all-to-all-start.8 = ((bf16[8,128,256]{2,1,0:T(8,128)(2,1)}), bf16[8,128,256]{2,1,0:T(8,128)(2,1)}, u32[]{:S(2)}, u32[]{:S(2)}) async-start(bf16[8,128,256]{2,1,0:T(8,128)(2,1)} %shard_map.167), calls=%async_computation.8 | async-start | bytes 1048576 | tf_op jit(solution)/shard_map/all_to_all | solution.py:205
  214.4 1.5 collective-permute-start.5
  215.9 4.2 %collective-permute-start.6 = (bf16[256,256]{1,0:T(8,128)(2,1)}, bf16[256,256]{1,0:T(8,128)(2,1)S(1)}, u32[]{:S(2)}, u32[]{:S(2)}) collective-permute-start(bf16[256,256]{1,0:T(8,128)(2,1)} %reduce_sum.73), channel_id=1, source_target_pairs={{0,0},{1,33},{2,66},{3,99},{4,132},{5,165},{6,198},{7,231},{8,16},... | collective-permute-start | bytes 393224 | tf_op jit(solution)/shard_map/ppermute | solution.py:324
  220.5 14.8 %collective-permute-done.6 = bf16[256,256]{1,0:T(8,128)(2,1)S(1)} collective-permute-done((bf16[256,256]{1,0:T(8,128)(2,1)}, bf16[256,256]{1,0:T(8,128)(2,1)S(1)}, u32[]{:S(2)}, u32[]{:S(2)}) %collective-permute-start.6) | collective-permute-done | bytes 131104 | tf_op jit(solution)/shard_map/ppermute | solution.py:324
  235.3 0.7 convert_element_type.55
  236.0 1.1 convert_reduce_fusion
  237.2 0.7 fusion.23
  (61 shorter events, 5.7 us)
Async XLA Ops:
  7.2 75.4 %copy-start = (bf16[5120,320]{0,1:T(8,128)(2,1)S(1)}, bf16[5120,320]{0,1:T(8,128)(2,1)}, u32[]{:S(2)}) copy-start(bf16[5120,320]{0,1:T(8,128)(2,1)} %param.20) | copy-start | bytes 9830404
  7.2 69.8 %all-gather.4.cloned.1.call-start = ((), (), s32[]{:S(2)}) async-start(), calls=%async_computation.9 | async-start | bytes 1474560 | tf_op jit(solution)/shard_map/all_gather | solution.py:237
  11.3 32.4 %all-to-all-start = ((bf16[16,40,1176]{2,1,0:T(8,128)(2,1)}), bf16[16,40,1176]{2,1,0:T(8,128)(2,1)}, u32[]{:S(2)}, u32[]{:S(2)}) async-start(bf16[16,40,1176]{2,1,0:T(8,128)(2,1)} %broadcast_in_dim.30), calls=%async_computation | async-start | bytes 3276800 | tf_op jit(solution)/shard_map/all_to_all | solution.py:240
  18.6 22.2 %collective-permute-start = (bf16[256,256]{1,0:T(8,128)(2,1)}, bf16[256,256]{1,0:T(8,128)(2,1)S(1)}, u32[]{:S(2)}, u32[]{:S(2)}) collective-permute-start(bf16[256,256]{1,0:T(8,128)(2,1)} %param.26), channel_id=1, source_target_pairs={{0,0},{1,32},{2,64},{3,96},{4,128},{5,160},{6,192},{7,224},{8,8},{... | collective-permute-start | bytes 393224 | tf_op jit(solution)/shard_map/ppermute | solution.py:248
  25.9 41.7 %copy-start.4 = (bf16[1,128,256]{2,1,0:T(8,128)(2,1)S(1)}, bf16[1,128,256]{2,1,0:T(8,128)(2,1)}, u32[]{:S(2)}) copy-start(bf16[1,128,256]{2,1,0:T(8,128)(2,1)} %param.27) | copy-start | bytes 196612
  40.8 2.8 %copy-start.3 = (bf16[256,256]{1,0:T(8,128)(2,1)}, bf16[256,256]{1,0:T(8,128)(2,1)S(1)}, u32[]{:S(2)}) copy-start(bf16[256,256]{1,0:T(8,128)(2,1)S(1)} %collective-permute-done) | copy-start | bytes 393220
  43.6 22.1 %all-to-all-start.1 = ((bf16[8,40,256]{2,1,0:T(8,128)(2,1)}), bf16[8,40,256]{2,1,0:T(8,128)(2,1)S(1)}, u32[]{:S(2)}, u32[]{:S(2)}) async-start(bf16[8,40,256]{2,1,0:T(8,128)(2,1)} %shard_map.165), calls=%async_computation.1 | async-start | bytes 327680 | tf_op jit(solution)/shard_map/all_to_all | solution.py:205
  56.3 86.7 %all-gather.6.cloned.1.call-start = ((), (), s32[]{:S(2)}) async-start(), calls=%async_computation.10 | async-start | bytes 10813440 | tf_op jit(solution)/shard_map/all_gather | solution.py:255
  67.5 5.1 %collective-permute-start.1 = (bf16[16,40,1176]{2,1,0:T(8,128)(2,1)}, bf16[16,40,1176]{2,1,0:T(8,128)(2,1)}, u32[]{:S(2)}, u32[]{:S(2)}) collective-permute-start(bf16[16,40,1176]{2,1,0:T(8,128)(2,1)} %all-to-all-done), channel_id=1, source_target_pairs={{0,8},{8,0},{16,24},{24,16},{32,40},{40,32},{48,56},{56,48},{64,72... | collective-permute-start | bytes 4515848 | tf_op jit(solution)/shard_map/ppermute | solution.py:30
  68.5 22.6 %all-to-all-start.2 = ((bf16[8,128,256]{2,1,0:T(8,128)(2,1)}), bf16[8,128,256]{2,1,0:T(8,128)(2,1)}, u32[]{:S(2)}, u32[]{:S(2)}) async-start(bf16[8,128,256]{2,1,0:T(8,128)(2,1)} %broadcast_in_dim.31), calls=%async_computation.2 | async-start | bytes 1048576 | tf_op jit(solution)/shard_map/all_to_all | solution.py:205
  81.3 0.7 copy-start.6
  81.3 0.7 copy-start.7
  82.0 0.7 copy-start.9
  84.2 7.9 %collective-permute-start.2 = (bf16[112,320]{1,0:T(8,128)(2,1)S(1)}, bf16[112,320]{1,0:T(8,128)(2,1)S(1)}, u32[]{:S(2)}, u32[]{:S(2)}) collective-permute-start(bf16[112,320]{1,0:T(8,128)(2,1)S(1)} %reshape.115), channel_id=1, source_target_pairs={{0,128},{128,0},{1,129},{129,1},{2,130},{130,2},{3,131},{131,3},{4... | collective-permute-start | bytes 215048 | tf_op jit(solution)/shard_map/ppermute | solution.py:34
  93.1 27.2 %all-to-all-start.3 = ((bf16[8,320,112]{2,1,0:T(8,128)(2,1)}), bf16[8,320,112]{2,1,0:T(8,128)(2,1)}, u32[]{:S(2)}, u32[]{:S(2)}) async-start(bf16[8,320,112]{2,1,0:T(8,128)(2,1)} %broadcast_in_dim.32), calls=%async_computation.3 | async-start | bytes 1310720 | tf_op jit(solution)/shard_map/all_to_all | solution.py:205
  101.5 24.9 %copy-start.10 = (s32[32]{0:T(128)S(1)}, s32[32]{0:T(128)}, u32[]{:S(2)}) copy-start(s32[32]{0:T(128)} %param.15) | copy-start | bytes 388
  101.5 37.3 %copy-start.8 = (s32[1,112]{1,0:T(1,128)S(1)}, s32[1,112]{1,0:T(1,128)}, u32[]{:S(2)}) copy-start(s32[1,112]{1,0:T(1,128)} %param.16) | copy-start | bytes 1348
  120.3 18.4 %all-to-all-start.4 = ((bf16[4,128,512]{2,1,0:T(8,128)(2,1)}), bf16[4,128,512]{2,1,0:T(8,128)(2,1)}, u32[]{:S(2)}, u32[]{:S(2)}) async-start(bf16[4,128,512]{2,1,0:T(8,128)(2,1)} %reshape.118), calls=%async_computation.4 | async-start | bytes 1048576 | tf_op jit(solution)/shard_map/all_to_all | solution.py:281
  138.8 18.7 %collective-permute-start.3 = (bf16[4,128,512]{2,1,0:T(8,128)(2,1)}, bf16[4,128,512]{2,1,0:T(8,128)(2,1)}, u32[]{:S(2)}, u32[]{:S(2)}) collective-permute-start(bf16[4,128,512]{2,1,0:T(8,128)(2,1)} %all-to-all-done.4.own_ref), channel_id=1, source_target_pairs={{0,8},{8,0},{16,24},{24,16},{32,40},{40,32},{48,56},{56,48},{64,72... | collective-permute-start | bytes 1572872 | tf_op jit(solution)/shard_map/ppermute | solution.py:30
  150.2 4.9 %copy-start.2 = (bf16[1,128,1024]{2,1,0:T(8,128)(2,1)S(1)}, bf16[1,128,1024]{2,1,0:T(8,128)(2,1)}, u32[]{:S(2)}) copy-start(bf16[1,128,1024]{2,1,0:T(8,128)(2,1)} %param.24) | copy-start | bytes 786436
  150.2 4.9 %copy-start.5 = (f32[1024]{0:T(1024)S(1)}, f32[1024]{0:T(1024)}, u32[]{:S(2)}) copy-start(f32[1024]{0:T(1024)} %param.25) | copy-start | bytes 12292
  172.1 42.0 %copy-start.1 = (bf16[128,1024]{1,0:T(8,128)(2,1)}, bf16[128,1024]{1,0:T(8,128)(2,1)S(1)}, u32[]{:S(2)}) copy-start(bf16[128,1024]{1,0:T(8,128)(2,1)S(1)} %get-tuple-element.38) | copy-start | bytes 786436
  172.1 1.4 collective-permute-start.4
  194.9 13.2 %all-to-all-start.7 = ((bf16[4,256,256]{2,1,0:T(8,128)(2,1)}), bf16[4,256,256]{2,1,0:T(8,128)(2,1)}, u32[]{:S(2)}, u32[]{:S(2)}) async-start(bf16[4,256,256]{2,1,0:T(8,128)(2,1)} %shard_map.169), calls=%async_computation.7 | async-start | bytes 1048576 | tf_op jit(solution)/shard_map/all_to_all | solution.py:320
  209.9 26.1 %all-to-all-start.8 = ((bf16[8,128,256]{2,1,0:T(8,128)(2,1)}), bf16[8,128,256]{2,1,0:T(8,128)(2,1)}, u32[]{:S(2)}, u32[]{:S(2)}) async-start(bf16[8,128,256]{2,1,0:T(8,128)(2,1)} %shard_map.167), calls=%async_computation.8 | async-start | bytes 1048576 | tf_op jit(solution)/shard_map/all_to_all | solution.py:205
  214.4 6.1 %collective-permute-start.5 = (bf16[112,1024]{1,0:T(8,128)(2,1)S(1)}, bf16[112,1024]{1,0:T(8,128)(2,1)S(1)}, u32[]{:S(2)}, u32[]{:S(2)}) collective-permute-start(bf16[112,1024]{1,0:T(8,128)(2,1)S(1)} %convolution_convert_fusion), channel_id=1, source_target_pairs={{0,128},{128,0},{1,129},{129,1},{2,130},{130,2},{3,131},{131,3},{4... | collective-permute-start | bytes 688136 | tf_op jit(solution)/shard_map/ppermute | solution.py:34
  215.9 19.4 %collective-permute-start.6 = (bf16[256,256]{1,0:T(8,128)(2,1)}, bf16[256,256]{1,0:T(8,128)(2,1)S(1)}, u32[]{:S(2)}, u32[]{:S(2)}) collective-permute-start(bf16[256,256]{1,0:T(8,128)(2,1)} %reduce_sum.73), channel_id=1, source_target_pairs={{0,0},{1,33},{2,66},{3,99},{4,132},{5,165},{6,198},{7,231},{8,16},... | collective-permute-start | bytes 393224 | tf_op jit(solution)/shard_map/ppermute | solution.py:324
Sparse Core Ops, SparseCore 0:
  10.4 47.7 all-gather.3
  67.7 73.5 all-gather.5

commit v3 on v2

--- a/solution.py
+++ b/solution.py
@@ -22,7 +22,7 @@
     [plane_index(x, y, core) for lo in range(2) for x in range(4) for y in (lo, lo + 2)]
     for core in range(2)
 ]
-SAME_X = [[plane_index(x, y, core) for y in range(4)] for x in range(4) for core in range(2)]
+SAME_X = [[plane_index(x, y, core) for y in range(4) for core in range(2)] for x in range(4)]
 SAME_Y = [[plane_index(x, y, core) for x in range(4)] for y in range(4) for core in range(2)]
 
 
@@ -38,7 +38,8 @@
     route = []
     for p in range(32):
         for t in range(N_TP):
-            route.append((p * N_TP + t, (t * 4 + p % 4) * N_TP + p // 4))
+            plane = p // 4
+            route.append((p * N_TP + t, ((t ^ plane) * 4 + p % 4) * N_TP + plane))
     return route
 
 
@@ -98,91 +99,81 @@
     )(hidden, gathered, bias[None])
 
 
-def block_product_kernel(left_ref, right_ref, out_ref):
+def block_product_kernel(plane_ref, left_ref, right_ref, out_ref):
     out_ref[0] = jnp.dot(
         left_ref[...], right_ref[0].reshape(1024, 256), preferred_element_type=F32
-    ).astype(out_ref.dtype)
-
-
-def block_product(left, gathered):
+    )
+
+
+def block_product(left, gathered, plane):
     rows = left.shape[0]
     return pl.pallas_call(
         block_product_kernel,
-        grid=(N_TP,),
-        in_specs=[
-            pl.BlockSpec((rows, 1024), lambda i: (0, 0)),
-            pl.BlockSpec((1, 4, 256, 256), lambda i: (i, 0, 0, 0)),
-        ],
-        out_specs=pl.BlockSpec((1, rows, 256), lambda i: (i, 0, 0)),
-        out_shape=jax.ShapeDtypeStruct((N_TP, rows, 256), BF),
+        grid_spec=pltpu.PrefetchScalarGridSpec(
+            num_scalar_prefetch=1,
+            grid=(N_TP,),
+            in_specs=[
+                pl.BlockSpec((rows, 1024), lambda i, plane: (0, 0)),
+                pl.BlockSpec((1, 4, 256, 256), lambda i, plane: (i, 0, 0, 0)),
+            ],
+            out_specs=pl.BlockSpec((1, rows, 256), lambda i, plane: (i ^ plane[0], 0, 0)),
+        ),
+        out_shape=jax.ShapeDtypeStruct((N_TP, rows, 256), F32),
         cost_estimate=pl.CostEstimate(
             flops=2 * rows * 1024 * 2048, bytes_accessed=4 << 20, transcendentals=0
         ),
-    )(left, gathered)
-
-
-def block_sum_kernel(left_ref, right_ref, out_ref, total_ref):
-    step = pl.program_id(0)
-    part = lax.dot_general(
-        right_ref[0].reshape(1024, 256),
-        left_ref[0],
-        (((1,), (1,)), ((), ())),
-        preferred_element_type=F32,
-    )
-
-    @pl.when(step == 0)
-    def _():
-        total_ref[...] = part
-
-    @pl.when(step > 0)
-    def _():
-        total_ref[...] += part
-
-    @pl.when(step == N_TP - 1)
-    def _():
-        out_ref[...] = total_ref[...].T
+    )(plane.astype(jnp.int32)[None], left, gathered)
+
+
+def block_sum_kernel(left_ref, right_ref, out_ref):
+    total = jnp.zeros(out_ref.shape, F32)
+    for t in range(N_TP):
+        total += lax.dot_general(
+            left_ref[t],
+            right_ref[t, 0],
+            (((1,), (1,)), ((), ())),
+            preferred_element_type=F32,
+        )
+    out_ref[...] = total
 
 
 def block_sum(left, gathered):
     rows = left.shape[1]
     return pl.pallas_call(
         block_sum_kernel,
-        grid=(N_TP,),
+        grid=(4,),
         in_specs=[
-            pl.BlockSpec((1, rows, 256), lambda i: (i, 0, 0)),
-            pl.BlockSpec((1, 4, 256, 256), lambda i: (i, 0, 0, 0)),
+            pl.BlockSpec((N_TP, rows, 256), lambda i: (0, 0, 0)),
+            pl.BlockSpec((N_TP, 1, 256, 256), lambda i: (0, i, 0, 0)),
         ],
-        out_specs=pl.BlockSpec((rows, 1024), lambda i: (0, 0)),
+        out_specs=pl.BlockSpec((rows, 256), lambda i: (0, i)),
         out_shape=jax.ShapeDtypeStruct((rows, 1024), F32),
-        scratch_shapes=[pltpu.VMEM((1024, rows), F32)],
         cost_estimate=pl.CostEstimate(
             flops=2 * rows * 1024 * 2048, bytes_accessed=4 << 20, transcendentals=0
         ),
     )(left, gathered)
 
 
-def line_product_kernel(normed_ref, own_ref, other_ref, out_ref):
-    total = jnp.zeros((512, 512), F32)
-    for side, cot_ref in enumerate((own_ref, other_ref)):
-        total += lax.dot_general(
-            normed_ref[:, side].reshape(512, 512),
-            cot_ref[...].reshape(512, 512),
-            (((0,), (0,)), ((), ())),
-            preferred_element_type=F32,
-        )
+def line_product_kernel(normed_ref, cot_ref, out_ref):
+    total = lax.dot_general(
+        normed_ref[...].reshape(1024, 512),
+        cot_ref[...].reshape(1024, 512),
+        (((0,), (0,)), ((), ())),
+        preferred_element_type=F32,
+    )
     for i in range(4):
         row, col = i // 2 * 256, i % 2 * 256
         out_ref[i] = total[row : row + 256, col : col + 256].astype(BF)
 
 
-def line_product(normed, own, other):
+def line_product(normed, cotangents):
     return pl.pallas_call(
         line_product_kernel,
         out_shape=jax.ShapeDtypeStruct((4, 256, 256), BF),
         cost_estimate=pl.CostEstimate(
             flops=2 * 1024 * 512 * 512, bytes_accessed=3 << 20, transcendentals=0
         ),
-    )(normed, own, other)
+    )(normed, cotangents)
 
 
 def flip_bits(blocks, number):
@@ -236,7 +227,11 @@
     rows = jnp.pad(rows, ((0, 0), (0, 16 - tokens), (0, 0))).reshape(MERGE_PATCHES * 16, -1)
     patch_all = lax.all_gather(rows, "tp", tiled=True)
 
-    columns = pe_weight.T
+    place = sec * 16 + dp
+    weight_block = lax.ppermute(kv_weight, ALL, weight_to_plane())
+    share = exchange_tp(take_share(w_out, place)).reshape(320, 256)
+
+    columns, _ = lax.optimization_barrier((pe_weight.T, share))
     mine = lax.all_to_all(
         jnp.broadcast_to(columns[None], (16,) + columns.shape),
         PLANE,
@@ -244,17 +239,10 @@
         0,
         axis_index_groups=SAME_CORE,
     )
-    place = sec * 16 + dp
-    weight_block = lax.ppermute(kv_weight, ALL, weight_to_plane())
-    share, weight_block, mine = lax.optimization_barrier(
-        (take_share(w_out, place), weight_block, mine)
-    )
-    share = exchange_tp(share).reshape(320, 256)
-
     shard = jnp.concatenate([weight_block, jnp.zeros((64, 256), BF), share], axis=0)
     gathered = lax.all_gather(shard, PLANE).reshape(8, 4, 640, 256)
 
-    cot_input, _ = lax.optimization_barrier((kv_cotangent[0], share))
+    cot_input, mine = lax.optimization_barrier((kv_cotangent[0], mine))
     cotangents = gather_tp(cot_input)
     other = swap_cores(mine)
     first = jnp.where(core == 0, mine, other)
@@ -275,11 +263,12 @@
     hidden, cotangents = lax.optimization_barrier((hidden, cotangents))
     hidden = gather_tp(hidden)
 
-    cot_line = flip_bits(cotangents, tp)
-    cot_line = cot_line.reshape(4, 2, 128, 256).transpose(0, 2, 1, 3).reshape(4, 128, 512)
+    cotangents = flip_bits(cotangents, tp)
+    cot_line = cotangents
+    cot_line = cot_line.reshape(4, 1, 2, 128, 256).transpose(0, 1, 3, 2, 4)
+    cot_line = jnp.broadcast_to(cot_line, (4, 2, 128, 2, 256)).reshape(8, 128, 512)
     cot_line, hidden = lax.optimization_barrier((cot_line, hidden))
     cot_line = lax.all_to_all(cot_line, PLANE, 0, 0, axis_index_groups=SAME_X)
-    cot_other = swap_cores(cot_line)
 
     hidden = hidden.reshape(N_TP, 8, 40, -1).transpose(1, 0, 2, 3).reshape(2560, -1).T
     vision = vision_product(hidden, gathered, b_out)
@@ -296,10 +285,31 @@
     normed_grad = block_sum(cotangents, gathered)
     scaled = normed_grad * rms_gain
     stats = jnp.stack([jnp.sum(combined * combined, axis=1), jnp.sum(scaled * combined, axis=1)])
-    stats, cot_line, cot_other = lax.optimization_barrier((stats, cot_line, cot_other))
+    stats, cot_line = lax.optimization_barrier((stats, cot_line))
     stats = jnp.sum(gather_tp(stats), axis=0)
     row_scale = lax.rsqrt(stats[0] / WIDTH + 1e-06)[:, None]
     row_dot = stats[1][:, None]
+
+    gained = combined * rms_gain
+    product = block_product(gained.astype(BF), gathered, tp)
+    row_scale, product = lax.optimization_barrier((row_scale, product))
+    normed = (gained * row_scale).astype(BF)
+    normed = normed.reshape(128, 2, 512).transpose(1, 0, 2)
+    normed_line = lax.all_to_all(
+        jnp.broadcast_to(normed[None], (4, 2, 128, 512)).reshape(8, 128, 512),
+        PLANE,
+        0,
+        0,
+        axis_index_groups=SAME_X,
+    )
+    block = line_product(normed_line, cot_line)
+    block = lax.all_to_all(block, PLANE, 0, 0, axis_index_groups=SAME_Y)
+    block = jnp.sum(block.astype(F32), axis=0).astype(BF)
+    kv_weight_grad = lax.ppermute(block, ALL, grad_from_plane()).astype(F32)
+
+    keys_values = lax.psum_scatter(product, "tp", scatter_dimension=0, tiled=True)[0]
+    keys_values = (keys_values * row_scale).astype(BF)
+
     seq_grad = (
         row_scale * scaled - combined * row_scale * row_scale * row_scale * row_dot / WIDTH
     ).astype(BF)
@@ -307,23 +317,6 @@
         selector_bf, seq_grad, (((0,), (0,)), ((), ())), preferred_element_type=F32
     ).astype(BF)
     vision_grad = swap_halves(image_grad)
-
-    gained = combined * rms_gain
-    normed = (gained * row_scale).astype(BF)
-    keep = jnp.where(core == 0, normed[:, :512], normed[:, 512:])
-    give = jnp.where(core == 0, normed[:, 512:], normed[:, :512])
-    pair = jnp.stack([keep, swap_cores(give)])
-    normed_line = lax.all_to_all(
-        jnp.broadcast_to(pair[None], (4,) + pair.shape), PLANE, 0, 0, axis_index_groups=SAME_X
-    )
-    block = line_product(normed_line, cot_line, cot_other)
-    block = lax.all_to_all(block, PLANE, 0, 0, axis_index_groups=SAME_Y)
-    product = block_product(gained.astype(BF), gathered)
-    block = jnp.sum(block.astype(F32), axis=0).astype(BF)
-    product, block = lax.optimization_barrier((product, block))
-    kv_weight_grad = lax.ppermute(block, ALL, grad_from_plane()).astype(F32)
-    keys_values = jnp.sum(exchange_tp(product).astype(F32), axis=0)
-    keys_values = (keys_values * row_scale).astype(BF)
     return (keys_values[None], seq_grad[None], vision_grad[None], kv_weight_grad)
 
 

time: 250 us -> 237 us (0.948); the launches traced: 245 us -> 235 us
  waiting for transfers between devices: 71.1 us -> 54.9 us
  blocking collectives: 30.6 us -> 45.8 us
  starting transfers between devices: 63.7 us -> 54.2 us
    all_to_all x2, blocking collectives: 30.6 us -> 45.8 us  [the longest x1 26.9 us: per_device(): lax.all_to_all(jnp.broadcast_to(columns[None], (16,) + columns.shape), PL...]
    all_to_all x1, waiting for transfers between devices: 11.1 us -> 0.01 us  [per_device(): cot_line = lax.all_to_all(cot_line, PLANE, 0, 0, axis_index_groups=SAME_X)]
    all_to_all x4, waiting for transfers between devices: 28.4 us -> 18.9 us  [exchange_tp(): return lax.all_to_all(blocks, 'tp', 0, 0)]
    all_to_all x1 -> x0, starting transfers between devices: 7.31 us -> none  [per_device(): lax.all_to_all(jnp.broadcast_to(columns[None], (16,) + columns.shape), PL...]
    ppermute x1, waiting for transfers between devices: 10.7 us -> 17.9 us  [per_device(): weight_block = lax.ppermute(kv_weight, ALL, weight_to_plane())]
    all_to_all x1, waiting for transfers between devices: 0.57 us -> 6.44 us  [per_device(): block = lax.all_to_all(block, PLANE, 0, 0, axis_index_groups=SAME_Y)]
    all_to_all x1, starting transfers between devices: 6.06 us -> 10.5 us  [per_device(): block = lax.all_to_all(block, PLANE, 0, 0, axis_index_groups=SAME_Y)]
    ppermute x1, waiting for transfers between devices: 14.8 us -> 11.4 us  [per_device(): kv_weight_grad = lax.ppermute(block, ALL, grad_from_plane()).astype(F32)]
  transfers between devices with their start and end apart: 16 -> 14, of which waited for: 11 -> 7; matrix products, arithmetic and copies ran while one was open for 13% -> 15% of each run, Pallas kernels for 9% -> 10%
where the time goes in v3:
time: 237 us; the launch traced here: 235 us
  waiting for transfers between devices  54.9 us (23%)
  starting transfers between devices  54.2 us (23%)
  blocking collectives  45.8 us (19%)
  Pallas kernels  23.9 us (10%)
  local copies, waits for them, and re-layouts  17.2 us (7%)
  other arithmetic  15.7 us (7%)
  between operations  14 us (6%)
  matrix products  9.14 us (4%)
    all_to_all x4, starting transfers between devices, exchange_tp(): return lax.all_to_all(blocks, 'tp', 0, 0)  27.2 us
    all_to_all x1, blocking collectives, per_device(): lax.all_to_all(jnp.broadcast_to(columns[None], (16,) + columns.shape), PL...  26.9 us
    all_to_all x4, waiting for transfers between devices, exchange_tp(): return lax.all_to_all(blocks, 'tp', 0, 0)  18.9 us
    all_to_all x1, blocking collectives, per_device(): lax.all_to_all(jnp.broadcast_to(normed[None], (4, 2, 128, 512)).reshape(8...  18.9 us
    ppermute x1, waiting for transfers between devices, per_device(): weight_block = lax.ppermute(kv_weight, ALL, weight_to_plane())  17.9 us
    ppermute x1, waiting for transfers between devices, per_device(): kv_weight_grad = lax.ppermute(block, ALL, grad_from_plane()).astype(F32)  11.4 us
    all_to_all x1, starting transfers between devices, per_device(): block = lax.all_to_all(block, PLANE, 0, 0, axis_index_groups=SAME_Y)  10.5 us
    pallas_call x1, Pallas kernels, block_product(): pl.pallas_call(block_product_kernel, grid_spec=pltpu.PrefetchScalarGridSp...  6.76 us
  transfers between devices with their start and end apart: 14, of which 7 were waited for; matrix products, arithmetic and copies ran while one was open for 15% of the time, Pallas kernels for 10%

profile of v3, /device:TPU:14, one launch (start us, length us, event | category | flops | bytes accessed | tf_op | source)
XLA Modules:
  0.0 234.9 jit_solution(1777616679037167212)
XLA Ops:
  7.2 1.1 reshape_squeeze.15
  8.4 0.7 pad.4.clone
  9.1 4.2 %shard_map.165 = bf16[8,40,256]{2,1,0:T(8,128)(2,1)} custom-call(s32[1]{0:T(128)} %bitcast.6.place_ref, bf16[320,8192]{1,0:T(8,128)(2,1)} %block_ref.1), custom_call_target="tpu_custom_call" | custom-call | bytes 327680 | tf_op jit(solution)/shard_map/pallas_call | solution.py:63
  13.3 8.5 %all-to-all-start = ((bf16[8,40,256]{2,1,0:T(8,128)(2,1)}), bf16[8,40,256]{2,1,0:T(8,128)(2,1)S(1)}, u32[]{:S(2)}, u32[]{:S(2)}) async-start(bf16[8,40,256]{2,1,0:T(8,128)(2,1)} %shard_map.165), calls=%async_computation | async-start | bytes 327680 | tf_op jit(solution)/shard_map/all_to_all | solution.py:196
  21.8 5.1 %collective-permute-start.2 = (bf16[256,256]{1,0:T(8,128)(2,1)}, bf16[256,256]{1,0:T(8,128)(2,1)}, u32[]{:S(2)}, u32[]{:S(2)}) collective-permute-start(bf16[256,256]{1,0:T(8,128)(2,1)} %param.26), channel_id=1, source_target_pairs={{0,0},{1,32},{2,64},{3,96},{4,128},{5,160},{6,192},{7,224},{8,8},{... | collective-permute-start | bytes 393224 | tf_op jit(solution)/shard_map/ppermute | solution.py:231
  26.9 17.9 %collective-permute-done.2 = bf16[256,256]{1,0:T(8,128)(2,1)} collective-permute-done((bf16[256,256]{1,0:T(8,128)(2,1)}, bf16[256,256]{1,0:T(8,128)(2,1)}, u32[]{:S(2)}, u32[]{:S(2)}) %collective-permute-start.2) | collective-permute-done | bytes 131104 | tf_op jit(solution)/shard_map/ppermute | solution.py:231
  44.9 1.8 pad_maximum_fusion.1
  46.8 26.9 %all_to_all.40 = bf16[16,40,1176]{2,1,0:T(8,128)(2,1)} all-to-all(bf16[16,40,1176]{2,1,0:T(8,128)(2,1)S(1)} %broadcast_in_dim.36), channel_id=1, replica_groups={{0,16,32,48,64,80,96,112,128,144,160,176,192,208,224,240},{8,24,40,56,7..., dimensions={0} | all-to-all | bytes 3010560 | tf_op jit(solution)/shard_map/all_to_all | solution.py:235
  73.8 0.9 broadcast_in_dim.37
  74.6 5.6 %all-to-all-start.2 = ((bf16[8,128,256]{2,1,0:T(8,128)(2,1)}), bf16[8,128,256]{2,1,0:T(8,128)(2,1)}, u32[]{:S(2)}, u32[]{:S(2)}) async-start(bf16[8,128,256]{2,1,0:T(8,128)(2,1)} %broadcast_in_dim.37), calls=%async_computation.2 | async-start | bytes 1048576 | tf_op jit(solution)/shard_map/all_to_all | solution.py:196
  80.2 2.2 select_bitcast_fusion.1
  82.4 2.1 pad_maximum_fusion
  84.6 4.4 %fusion.33 = (f32[512]{0:T(512)S(1)}, f32[512,1280]{1,0:T(8,128)S(1)}) fusion(bf16[512,1176]{1,0:T(8,128)(2,1)} %all-gather.4.cloned.1.call-done, bf16[1280,1176]{1,0:T(8,128)(2,1)} %bitcast.65), kind=kOutput, calls=%fused_computation.61 | convolution fusion | flops 1542061568 | bytes 6838272 | tf_op jit(solution)/shard_map/dot_general | solution.py:251
  90.4 1.3 fusion.13
  91.9 1.6 collective-permute-start.1
  93.5 5.0 %all-to-all-done.2 = bf16[8,128,256]{2,1,0:T(8,128)(2,1)} async-done(((bf16[8,128,256]{2,1,0:T(8,128)(2,1)}), bf16[8,128,256]{2,1,0:T(8,128)(2,1)}, u32[]{:S(2)}, u32[]{:S(2)}) %all-to-all-start.2) | async-done | bytes 524320 | tf_op jit(solution)/shard_map/all_to_all | solution.py:196
  98.8 0.9 broadcast_in_dim.40
  99.7 7.2 %all-to-all-start.3 = ((bf16[8,320,112]{2,1,0:T(8,128)(2,1)}), bf16[8,320,112]{2,1,0:T(8,128)(2,1)}, u32[]{:S(2)}, u32[]{:S(2)}) async-start(bf16[8,320,112]{2,1,0:T(8,128)(2,1)} %broadcast_in_dim.40), calls=%async_computation.3 | async-start | bytes 1310720 | tf_op jit(solution)/shard_map/all_to_all | solution.py:196
  106.9 1.3 reverse_select_fusion.2
  108.5 0.8 copy-done.1
  109.8 1.5 broadcast_in_dim.39
  111.3 2.6 %reshape.114 = bf16[8,128,512]{2,1,0:T(8,128)(2,1)} reshape(bf16[4,2,128,2,256]{4,3,2,1,0:T(2,128)(2,1)} %broadcast_in_dim.39) | data formatting | bytes 2097152 | tf_op jit(solution)/shard_map/reshape | solution.py:269
  113.9 13.0 %all-to-all-done.3 = bf16[8,320,112]{2,1,0:T(8,128)(2,1)} async-done(((bf16[8,320,112]{2,1,0:T(8,128)(2,1)}), bf16[8,320,112]{2,1,0:T(8,128)(2,1)}, u32[]{:S(2)}, u32[]{:S(2)}) %all-to-all-start.3) | async-done | bytes 573472 | tf_op jit(solution)/shard_map/all_to_all | solution.py:196
  126.9 5.2 %all-to-all-start.4 = ((bf16[8,128,512]{2,1,0:T(8,128)(2,1)}), bf16[8,128,512]{2,1,0:T(8,128)(2,1)}, u32[]{:S(2)}, u32[]{:S(2)}) async-start(bf16[8,128,512]{2,1,0:T(8,128)(2,1)} %reshape.114), calls=%async_computation.4 | async-start | bytes 2097152 | tf_op jit(solution)/shard_map/all_to_all | solution.py:271
  132.6 0.6 iota_compare_fusion.1
  133.4 2.0 copy.48
  135.4 2.2 copy.49
  137.6 4.9 %shard_map.167 = f32[128,1024]{1,0:T(8,128)} custom-call(bf16[8,128,256]{2,1,0:T(8,128)(2,1)} %bitcast.63, bf16[8,4,640,256]{3,2,1,0:T(8,128)(2,1)} %bitcast.58), custom_call_target="tpu_custom_call" | custom-call | flops 536870912 | bytes 4194304 | tf_op jit(solution)/shard_map/pallas_call | solution.py:142
  142.5 4.9 %shard_map.166 = bf16[112,1024]{1,0:T(8,128)(2,1)} custom-call(bf16[112,2560]{1,0:T(8,128)(2,1)} %bitcast.67, bf16[8,4,640,256]{3,2,1,0:T(8,128)(2,1)} %bitcast.59, f32[1,1024]{1,0:T(1,128)} %bitcast.85), custom_call_target="tpu_custom_call" | custom-call | flops 587202560 | bytes 5242880 | tf_op jit(solution)/shard_map/pallas_call | solution.py:86
  147.4 2.4 %multiply_reduce_fusion.2 = (f32[128]{0:T(128)S(1)}, f32[128]{0:T(128)S(1)}, bf16[128,1024]{1,0:T(8,128)(2,1)}, f32[128,1024]{1,0:T(8,128)}) fusion(f32[128,1024]{1,0:T(8,128)} %shard_map.167, f32[1024]{0:T(1024)S(1)} %copy-done.6, bf16[1,128,1024]{2,1,0:T(8,128)(2,1)S(1)} %copy-done.3, bf16[112,1024]{1,0:T(8,128)(2,1)} %shard_map.166, ...), kind=kOutput, calls=%fused_computation.23 | convolution fusion | flops 30568192 | bytes 1808048 | tf_op jit(solution)/shard_map/dot_general | solution.py:281
  149.9 0.6 broadcast_in_dim.43
  150.5 6.0 %all-to-all-start.5 = ((f32[8,2,128]{2,1,0:T(2,128)}), f32[8,2,128]{2,1,0:T(2,128)S(1)}, u32[]{:S(2)}, u32[]{:S(2)}) async-start(f32[8,2,128]{2,1,0:T(2,128)} %broadcast_in_dim.43), calls=%async_computation.5 | async-start | bytes 16384 | tf_op jit(solution)/shard_map/all_to_all | solution.py:196
  156.5 6.8 %shard_map.168 = f32[8,128,256]{2,1,0:T(8,128)} custom-call(s32[1]{0:T(128)} %bitcast.34.plane_ref, bf16[128,1024]{1,0:T(8,128)(2,1)} %get-tuple-element.36.left_ref, bf16[8,4,640,256]{3,2,1,0:T(8,128)(2,1)} %bitcast.60), custom_call_target="tpu_custom_call" | custom-call | flops 536870912 | bytes 4194304 | tf_op jit(solution)/shard_map/pallas_call | solution.py:110
  163.3 0.9 all-to-all-done.5
  164.2 2.2 multiply_convert_fusion
  166.5 1.1 reshape.119
  167.8 18.9 %all_to_all.41.normed_ref = bf16[8,128,512]{2,1,0:T(8,128)(2,1)} all-to-all(bf16[8,128,512]{2,1,0:T(8,128)(2,1)S(1)} %bitcast.64), channel_id=1, replica_groups={{0,8,128,136,16,24,144,152},{32,40,160,168,48,56,176,184},{64,72,192,20..., dimensions={0} | all-to-all | bytes 2097152 | tf_op jit(solution)/shard_map/all_to_all | solution.py:298
  186.6 3.1 %shard_map.169 = bf16[4,256,256]{2,1,0:T(8,128)(2,1)} custom-call(bf16[8,128,512]{2,1,0:T(8,128)(2,1)} %all_to_all.41.normed_ref, bf16[8,128,512]{2,1,0:T(8,128)(2,1)} %all-to-all-done.4.cot_ref), custom_call_target="tpu_custom_call" | custom-call | flops 536870912 | bytes 3145728 | tf_op jit(solution)/shard_map/pallas_call | solution.py:170
  189.7 10.5 %all-to-all-start.7 = ((bf16[4,256,256]{2,1,0:T(8,128)(2,1)}), bf16[4,256,256]{2,1,0:T(8,128)(2,1)}, u32[]{:S(2)}, u32[]{:S(2)}) async-start(bf16[4,256,256]{2,1,0:T(8,128)(2,1)} %shard_map.169), calls=%async_computation.8 | async-start | bytes 1048576 | tf_op jit(solution)/shard_map/all_to_all | solution.py:306
  200.2 1.0 convolution_convert_fusion
  201.1 1.4 collective-permute-start.3
  202.6 6.4 %all-to-all-done.7 = bf16[4,256,256]{2,1,0:T(8,128)(2,1)} async-done(((bf16[4,256,256]{2,1,0:T(8,128)(2,1)}), bf16[4,256,256]{2,1,0:T(8,128)(2,1)}, u32[]{:S(2)}, u32[]{:S(2)}) %all-to-all-start.7) | async-done | bytes 524320 | tf_op jit(solution)/shard_map/all_to_all | solution.py:306
  209.0 1.8 reduce_sum.62
  210.8 3.1 %collective-permute-start.4 = (bf16[256,256]{1,0:T(8,128)(2,1)}, bf16[256,256]{1,0:T(8,128)(2,1)S(1)}, u32[]{:S(2)}, u32[]{:S(2)}) collective-permute-start(bf16[256,256]{1,0:T(8,128)(2,1)} %reduce_sum.62), channel_id=1, source_target_pairs={{0,0},{1,33},{2,66},{3,99},{4,132},{5,165},{6,198},{7,231},{8,16},... | collective-permute-start | bytes 393224 | tf_op jit(solution)/shard_map/ppermute | solution.py:308
  213.9 11.4 %collective-permute-done.4 = bf16[256,256]{1,0:T(8,128)(2,1)S(1)} collective-permute-done((bf16[256,256]{1,0:T(8,128)(2,1)}, bf16[256,256]{1,0:T(8,128)(2,1)S(1)}, u32[]{:S(2)}, u32[]{:S(2)}) %collective-permute-start.4) | collective-permute-done | bytes 131104 | tf_op jit(solution)/shard_map/ppermute | solution.py:308
  225.4 0.7 convert_element_type.45
  226.1 1.6 multiply_convert_fusion.2
  227.7 0.7 copy.59
  (60 shorter events, 3.7 us)
Async XLA Ops:
  7.2 83.1 %copy-start = (bf16[5120,320]{0,1:T(8,128)(2,1)S(1)}, bf16[5120,320]{0,1:T(8,128)(2,1)}, u32[]{:S(2)}) copy-start(bf16[5120,320]{0,1:T(8,128)(2,1)} %param.20) | copy-start | bytes 9830404
  7.2 77.4 %all-gather.4.cloned.1.call-start = ((), (), s32[]{:S(2)}) async-start(), calls=%async_computation.9 | async-start | bytes 1474560 | tf_op jit(solution)/shard_map/all_gather | solution.py:228
  9.1 37.6 %copy-start.4 = (bf16[1176,40]{0,1:T(8,128)(2,1)S(1)}, bf16[1176,40]{0,1:T(8,128)(2,1)}, u32[]{:S(2)}) copy-start(bf16[1176,40]{0,1:T(8,128)(2,1)} %param.17) | copy-start | bytes 282244
  13.3 31.6 %all-to-all-start = ((bf16[8,40,256]{2,1,0:T(8,128)(2,1)}), bf16[8,40,256]{2,1,0:T(8,128)(2,1)S(1)}, u32[]{:S(2)}, u32[]{:S(2)}) async-start(bf16[8,40,256]{2,1,0:T(8,128)(2,1)} %shard_map.165), calls=%async_computation | async-start | bytes 327680 | tf_op jit(solution)/shard_map/all_to_all | solution.py:196
  21.8 115.8 %all-gather.6.cloned.1.call-start = ((), (), s32[]{:S(2)}) async-start(), calls=%async_computation.11 | async-start | bytes 10813440 | tf_op jit(solution)/shard_map/all_gather | solution.py:243
  21.8 23.1 %collective-permute-start.2 = (bf16[256,256]{1,0:T(8,128)(2,1)}, bf16[256,256]{1,0:T(8,128)(2,1)}, u32[]{:S(2)}, u32[]{:S(2)}) collective-permute-start(bf16[256,256]{1,0:T(8,128)(2,1)} %param.26), channel_id=1, source_target_pairs={{0,0},{1,32},{2,64},{3,96},{4,128},{5,160},{6,192},{7,224},{8,8},{... | collective-permute-start | bytes 393224 | tf_op jit(solution)/shard_map/ppermute | solution.py:231
  46.7 27.1 %copy-start.5 = (bf16[1,128,256]{2,1,0:T(8,128)(2,1)S(1)}, bf16[1,128,256]{2,1,0:T(8,128)(2,1)}, u32[]{:S(2)}) copy-start(bf16[1,128,256]{2,1,0:T(8,128)(2,1)} %param.27) | copy-start | bytes 196612
  73.8 6.5 %collective-permute-start = (bf16[16,40,1176]{2,1,0:T(8,128)(2,1)}, bf16[16,40,1176]{2,1,0:T(8,128)(2,1)}, u32[]{:S(2)}, u32[]{:S(2)}) collective-permute-start(bf16[16,40,1176]{2,1,0:T(8,128)(2,1)} %all_to_all.40), channel_id=1, source_target_pairs={{0,8},{8,0},{16,24},{24,16},{32,40},{40,32},{48,56},{56,48},{64,72... | collective-permute-start | bytes 4515848 | tf_op jit(solution)/shard_map/ppermute | solution.py:30
  74.6 23.9 %all-to-all-start.2 = ((bf16[8,128,256]{2,1,0:T(8,128)(2,1)}), bf16[8,128,256]{2,1,0:T(8,128)(2,1)}, u32[]{:S(2)}, u32[]{:S(2)}) async-start(bf16[8,128,256]{2,1,0:T(8,128)(2,1)} %broadcast_in_dim.37), calls=%async_computation.2 | async-start | bytes 1048576 | tf_op jit(solution)/shard_map/all_to_all | solution.py:196
  89.0 0.7 copy-start.7
  89.0 0.7 copy-start.8
  89.7 0.7 copy-start.10
  91.9 6.8 %collective-permute-start.1 = (bf16[112,320]{1,0:T(8,128)(2,1)S(1)}, bf16[112,320]{1,0:T(8,128)(2,1)S(1)}, u32[]{:S(2)}, u32[]{:S(2)}) collective-permute-start(bf16[112,320]{1,0:T(8,128)(2,1)S(1)} %reshape.112), channel_id=1, source_target_pairs={{0,128},{128,0},{1,129},{129,1},{2,130},{130,2},{3,131},{131,3},{4... | collective-permute-start | bytes 215048 | tf_op jit(solution)/shard_map/ppermute | solution.py:34
  99.7 27.1 %all-to-all-start.3 = ((bf16[8,320,112]{2,1,0:T(8,128)(2,1)}), bf16[8,320,112]{2,1,0:T(8,128)(2,1)}, u32[]{:S(2)}, u32[]{:S(2)}) async-start(bf16[8,320,112]{2,1,0:T(8,128)(2,1)} %broadcast_in_dim.40), calls=%async_computation.3 | async-start | bytes 1310720 | tf_op jit(solution)/shard_map/all_to_all | solution.py:196
  108.5 0.8 copy-start.1
  109.8 22.3 %copy-start.11 = (s32[32]{0:T(128)S(1)}, s32[32]{0:T(128)}, u32[]{:S(2)}) copy-start(s32[32]{0:T(128)} %param.15) | copy-start | bytes 388
  109.8 23.5 %copy-start.9 = (s32[1,112]{1,0:T(1,128)S(1)}, s32[1,112]{1,0:T(1,128)}, u32[]{:S(2)}) copy-start(s32[1,112]{1,0:T(1,128)} %param.16) | copy-start | bytes 1348
  126.9 23.0 %all-to-all-start.4 = ((bf16[8,128,512]{2,1,0:T(8,128)(2,1)}), bf16[8,128,512]{2,1,0:T(8,128)(2,1)}, u32[]{:S(2)}, u32[]{:S(2)}) async-start(bf16[8,128,512]{2,1,0:T(8,128)(2,1)} %reshape.114), calls=%async_computation.4 | async-start | bytes 2097152 | tf_op jit(solution)/shard_map/all_to_all | solution.py:271
  142.5 4.9 %copy-start.3 = (bf16[1,128,1024]{2,1,0:T(8,128)(2,1)S(1)}, bf16[1,128,1024]{2,1,0:T(8,128)(2,1)}, u32[]{:S(2)}) copy-start(bf16[1,128,1024]{2,1,0:T(8,128)(2,1)} %param.24) | copy-start | bytes 786436
  142.5 4.9 %copy-start.6 = (f32[1024]{0:T(1024)S(1)}, f32[1024]{0:T(1024)}, u32[]{:S(2)}) copy-start(f32[1024]{0:T(1024)} %param.25) | copy-start | bytes 12292
  150.5 13.7 %all-to-all-start.5 = ((f32[8,2,128]{2,1,0:T(2,128)}), f32[8,2,128]{2,1,0:T(2,128)S(1)}, u32[]{:S(2)}, u32[]{:S(2)}) async-start(f32[8,2,128]{2,1,0:T(2,128)} %broadcast_in_dim.43), calls=%async_computation.5 | async-start | bytes 16384 | tf_op jit(solution)/shard_map/all_to_all | solution.py:196
  156.4 69.7 %reduce-scatter.2.cloned.1.call-start = ((), (), s32[]{:S(2)}) async-start(), calls=%async_computation.10 | async-start | bytes 1179648 | tf_op jit(solution)/shard_map/reduce_scatter | solution.py:310
  167.7 32.5 %copy-start.2 = (bf16[128,1024]{1,0:T(8,128)(2,1)S(1)}, bf16[128,1024]{1,0:T(8,128)(2,1)}, u32[]{:S(2)}) copy-start(bf16[128,1024]{1,0:T(8,128)(2,1)} %get-tuple-element.35) | copy-start | bytes 786436
  189.7 19.3 %all-to-all-start.7 = ((bf16[4,256,256]{2,1,0:T(8,128)(2,1)}), bf16[4,256,256]{2,1,0:T(8,128)(2,1)}, u32[]{:S(2)}, u32[]{:S(2)}) async-start(bf16[4,256,256]{2,1,0:T(8,128)(2,1)} %shard_map.169), calls=%async_computation.8 | async-start | bytes 1048576 | tf_op jit(solution)/shard_map/all_to_all | solution.py:306
  201.1 12.8 %collective-permute-start.3 = (bf16[112,1024]{1,0:T(8,128)(2,1)}, bf16[112,1024]{1,0:T(8,128)(2,1)S(1)}, u32[]{:S(2)}, u32[]{:S(2)}) collective-permute-start(bf16[112,1024]{1,0:T(8,128)(2,1)} %convolution_convert_fusion), channel_id=1, source_target_pairs={{0,128},{128,0},{1,129},{129,1},{2,130},{130,2},{3,131},{131,3},{4... | collective-permute-start | bytes 688136 | tf_op jit(solution)/shard_map/ppermute | solution.py:34
  210.8 14.5 %collective-permute-start.4 = (bf16[256,256]{1,0:T(8,128)(2,1)}, bf16[256,256]{1,0:T(8,128)(2,1)S(1)}, u32[]{:S(2)}, u32[]{:S(2)}) collective-permute-start(bf16[256,256]{1,0:T(8,128)(2,1)} %reduce_sum.62), channel_id=1, source_target_pairs={{0,0},{1,33},{2,66},{3,99},{4,132},{5,165},{6,198},{7,231},{8,16},... | collective-permute-start | bytes 393224 | tf_op jit(solution)/shard_map/ppermute | solution.py:308
Sparse Core Ops, SparseCore 0:
  10.4 48.7 all-gather.3
  61.1 72.9 all-gather.5
  164.4 44.1 reduce-scatter.1

commit v4 on v3

--- a/solution.py
+++ b/solution.py
@@ -75,10 +75,12 @@
     )(place.astype(jnp.int32)[None], weight)
 
 
-def vision_kernel(left_ref, right_ref, bias_ref, out_ref):
-    right = right_ref[:, 0].reshape(left_ref.shape[1], -1)
-    total = jnp.dot(left_ref[...], right, preferred_element_type=F32) + bias_ref[...]
-    out_ref[...] = total.astype(BF)
+def vision_kernel(left_ref, most_ref, rest_ref, bias_ref, out_ref):
+    most = most_ref[:, 0].reshape(2048, 256)
+    rest = rest_ref[:, 0].reshape(512, 256)
+    total = jnp.dot(left_ref[:, :2048], most, preferred_element_type=F32)
+    total += jnp.dot(left_ref[:, 2048:], rest, preferred_element_type=F32)
+    out_ref[...] = (total + bias_ref[...]).astype(BF)
 
 
 def vision_product(hidden, gathered, bias):
@@ -88,7 +90,8 @@
         grid=(4,),
         in_specs=[
             pl.BlockSpec((rows, depth), lambda i: (0, 0)),
-            pl.BlockSpec((8, 1, 320, 256), lambda i: (0, i, 1, 0)),
+            pl.BlockSpec((8, 1, 256, 256), lambda i: (0, i, 1, 0)),
+            pl.BlockSpec((8, 1, 64, 256), lambda i: (0, i, 8, 0)),
             pl.BlockSpec((1, 256), lambda i: (0, i)),
         ],
         out_specs=pl.BlockSpec((rows, 256), lambda i: (0, i)),
@@ -96,7 +99,7 @@
         cost_estimate=pl.CostEstimate(
             flops=2 * rows * depth * 1024, bytes_accessed=2 * depth * 1024, transcendentals=0
         ),
-    )(hidden, gathered, bias[None])
+    )(hidden, gathered, gathered, bias[None])
 
 
 def block_product_kernel(plane_ref, left_ref, right_ref, out_ref):
@@ -239,8 +242,8 @@
         0,
         axis_index_groups=SAME_CORE,
     )
-    shard = jnp.concatenate([weight_block, jnp.zeros((64, 256), BF), share], axis=0)
-    gathered = lax.all_gather(shard, PLANE).reshape(8, 4, 640, 256)
+    shard = jnp.concatenate([weight_block, share], axis=0)
+    gathered = lax.all_gather(shard, PLANE).reshape(8, 4, 576, 256)
 
     cot_input, mine = lax.optimization_barrier((kv_cotangent[0], mine))
     cotangents = gather_tp(cot_input)
@@ -270,7 +273,10 @@
     cot_line, hidden = lax.optimization_barrier((cot_line, hidden))
     cot_line = lax.all_to_all(cot_line, PLANE, 0, 0, axis_index_groups=SAME_X)
 
-    hidden = hidden.reshape(N_TP, 8, 40, -1).transpose(1, 0, 2, 3).reshape(2560, -1).T
+    hidden = hidden.reshape(N_TP, 8, 40, -1).transpose(1, 0, 2, 3).reshape(8, 320, -1)
+    hidden = jnp.concatenate(
+        [hidden[:, :256].reshape(2048, -1), hidden[:, 256:].reshape(512, -1)], axis=0
+    ).T
     vision = vision_product(hidden, gathered, b_out)
 
     line_index = jnp.arange(128)

time: 237 us -> 232 us (0.979)
  starting transfers between devices: 54.2 us -> 49.8 us
  waiting for transfers between devices: 54.9 us -> 50.6 us
    all_to_all x1, starting transfers between devices: 10.5 us -> 6.39 us  [per_device(): block = lax.all_to_all(block, PLANE, 0, 0, axis_index_groups=SAME_Y)]
    all_to_all x4, starting transfers between devices: 27.2 us -> 24.5 us  [exchange_tp(): return lax.all_to_all(blocks, 'tp', 0, 0)]
  transfers between devices with their start and end apart: 14 -> 14, of which waited for: 7 -> 6; matrix products, arithmetic and copies ran while one was open for 15% -> 16% of each run, Pallas kernels for 10% -> 10%
where the time goes in v4:
time: 232 us; the launch traced here: 228 us
  waiting for transfers between devices  50.6 us (22%)
  starting transfers between devices  49.8 us (21%)
  blocking collectives  46.4 us (20%)
  Pallas kernels  23.8 us (10%)
  other arithmetic  17.3 us (7%)
  local copies, waits for them, and re-layouts  17.1 us (7%)
  between operations  14 us (6%)
  matrix products  9.12 us (4%)
    all_to_all x1, blocking collectives, per_device(): lax.all_to_all(jnp.broadcast_to(columns[None], (16,) + columns.shape), PL...  26.9 us
    all_to_all x4, starting transfers between devices, exchange_tp(): return lax.all_to_all(blocks, 'tp', 0, 0)  24.5 us
    all_to_all x1, blocking collectives, per_device(): lax.all_to_all(jnp.broadcast_to(normed[None], (4, 2, 128, 512)).reshape(8...  19.5 us
    ppermute x1, waiting for transfers between devices, per_device(): weight_block = lax.ppermute(kv_weight, ALL, weight_to_plane())  18 us
    all_to_all x4, waiting for transfers between devices, exchange_tp(): return lax.all_to_all(blocks, 'tp', 0, 0)  17.5 us
    ppermute x1, waiting for transfers between devices, per_device(): kv_weight_grad = lax.ppermute(block, ALL, grad_from_plane()).astype(F32)  10 us
    pallas_call x1, Pallas kernels, block_product(): pl.pallas_call(block_product_kernel, grid_spec=pltpu.PrefetchScalarGridSp...  6.76 us
    all_to_all x1, starting transfers between devices, per_device(): block = lax.all_to_all(block, PLANE, 0, 0, axis_index_groups=SAME_Y)  6.39 us
  transfers between devices with their start and end apart: 14, of which 6 were waited for; matrix products, arithmetic and copies ran while one was open for 16% of the time, Pallas kernels for 10%

profile of v4, /device:TPU:14, one launch (start us, length us, event | category | flops | bytes accessed | tf_op | source)
XLA Modules:
  0.0 228.3 jit_solution(14709229749413341229)
XLA Ops:
  7.2 1.1 reshape_squeeze.15
  8.4 0.7 pad.4.clone
  9.1 4.2 %shard_map.165 = bf16[8,40,256]{2,1,0:T(8,128)(2,1)} custom-call(s32[1]{0:T(128)} %bitcast.6.place_ref, bf16[320,8192]{1,0:T(8,128)(2,1)} %block_ref.1), custom_call_target="tpu_custom_call" | custom-call | bytes 327680 | tf_op jit(solution)/shard_map/pallas_call | solution.py:63
  13.3 8.5 %all-to-all-start = ((bf16[8,40,256]{2,1,0:T(8,128)(2,1)}), bf16[8,40,256]{2,1,0:T(8,128)(2,1)S(1)}, u32[]{:S(2)}, u32[]{:S(2)}) async-start(bf16[8,40,256]{2,1,0:T(8,128)(2,1)} %shard_map.165), calls=%async_computation | async-start | bytes 327680 | tf_op jit(solution)/shard_map/all_to_all | solution.py:199
  21.8 5.1 %collective-permute-start.2 = (bf16[256,256]{1,0:T(8,128)(2,1)}, bf16[256,256]{1,0:T(8,128)(2,1)}, u32[]{:S(2)}, u32[]{:S(2)}) collective-permute-start(bf16[256,256]{1,0:T(8,128)(2,1)} %param.26), channel_id=1, source_target_pairs={{0,0},{1,32},{2,64},{3,96},{4,128},{5,160},{6,192},{7,224},{8,8},{... | collective-permute-start | bytes 393224 | tf_op jit(solution)/shard_map/ppermute | solution.py:234
  26.9 18.0 %collective-permute-done.2 = bf16[256,256]{1,0:T(8,128)(2,1)} collective-permute-done((bf16[256,256]{1,0:T(8,128)(2,1)}, bf16[256,256]{1,0:T(8,128)(2,1)}, u32[]{:S(2)}, u32[]{:S(2)}) %collective-permute-start.2) | collective-permute-done | bytes 131104 | tf_op jit(solution)/shard_map/ppermute | solution.py:234
  44.9 1.6 pad_maximum_fusion.1
  46.7 26.9 %all_to_all.40 = bf16[16,40,1176]{2,1,0:T(8,128)(2,1)} all-to-all(bf16[16,40,1176]{2,1,0:T(8,128)(2,1)S(1)} %broadcast_in_dim.34), channel_id=1, replica_groups={{0,16,32,48,64,80,96,112,128,144,160,176,192,208,224,240},{8,24,40,56,7..., dimensions={0} | all-to-all | bytes 3010560 | tf_op jit(solution)/shard_map/all_to_all | solution.py:238
  73.6 0.8 broadcast_in_dim.35
  74.4 5.6 %all-to-all-start.2 = ((bf16[8,128,256]{2,1,0:T(8,128)(2,1)}), bf16[8,128,256]{2,1,0:T(8,128)(2,1)}, u32[]{:S(2)}, u32[]{:S(2)}) async-start(bf16[8,128,256]{2,1,0:T(8,128)(2,1)} %broadcast_in_dim.35), calls=%async_computation.2 | async-start | bytes 1048576 | tf_op jit(solution)/shard_map/all_to_all | solution.py:199
  80.0 2.2 select_bitcast_fusion.1
  82.2 2.0 pad_maximum_fusion
  84.2 4.4 %fusion.33 = (f32[512]{0:T(512)S(1)}, f32[512,1280]{1,0:T(8,128)S(1)}) fusion(bf16[512,1176]{1,0:T(8,128)(2,1)} %all-gather.4.cloned.1.call-done, bf16[1280,1176]{1,0:T(8,128)(2,1)} %bitcast.69), kind=kOutput, calls=%fused_computation.62 | convolution fusion | flops 1542061568 | bytes 6838272 | tf_op jit(solution)/shard_map/dot_general | solution.py:254
  90.0 1.3 fusion.13
  91.6 1.6 collective-permute-start.1
  93.2 5.1 %all-to-all-done.2 = bf16[8,128,256]{2,1,0:T(8,128)(2,1)} async-done(((bf16[8,128,256]{2,1,0:T(8,128)(2,1)}), bf16[8,128,256]{2,1,0:T(8,128)(2,1)}, u32[]{:S(2)}, u32[]{:S(2)}) %all-to-all-start.2) | async-done | bytes 524320 | tf_op jit(solution)/shard_map/all_to_all | solution.py:199
  98.5 1.0 broadcast_in_dim.38
  99.4 7.2 %all-to-all-start.3 = ((bf16[8,320,112]{2,1,0:T(8,128)(2,1)}), bf16[8,320,112]{2,1,0:T(8,128)(2,1)}, u32[]{:S(2)}, u32[]{:S(2)}) async-start(bf16[8,320,112]{2,1,0:T(8,128)(2,1)} %broadcast_in_dim.38), calls=%async_computation.3 | async-start | bytes 1310720 | tf_op jit(solution)/shard_map/all_to_all | solution.py:199
  107.8 1.3 reverse_select_fusion.2
  109.4 0.8 copy-done.1
  110.8 1.5 broadcast_in_dim.37
  112.3 2.5 %reshape.120 = bf16[8,128,512]{2,1,0:T(8,128)(2,1)} reshape(bf16[4,2,128,2,256]{4,3,2,1,0:T(2,128)(2,1)} %broadcast_in_dim.37) | data formatting | bytes 2097152 | tf_op jit(solution)/shard_map/reshape | solution.py:272
  114.8 11.6 %all-to-all-done.3 = bf16[8,320,112]{2,1,0:T(8,128)(2,1)} async-done(((bf16[8,320,112]{2,1,0:T(8,128)(2,1)}), bf16[8,320,112]{2,1,0:T(8,128)(2,1)}, u32[]{:S(2)}, u32[]{:S(2)}) %all-to-all-start.3) | async-done | bytes 573472 | tf_op jit(solution)/shard_map/all_to_all | solution.py:199
  126.4 5.5 %all-to-all-start.4 = ((bf16[8,128,512]{2,1,0:T(8,128)(2,1)}), bf16[8,128,512]{2,1,0:T(8,128)(2,1)}, u32[]{:S(2)}, u32[]{:S(2)}) async-start(bf16[8,128,512]{2,1,0:T(8,128)(2,1)} %reshape.120), calls=%async_computation.4 | async-start | bytes 2097152 | tf_op jit(solution)/shard_map/all_to_all | solution.py:274
  132.0 1.2 copy.51
  133.2 0.8 slice.41
  134.0 2.0 copy.56
  136.2 1.9 maximum_bitcast_fusion.left_ref
  138.0 4.9 %shard_map.167 = f32[128,1024]{1,0:T(8,128)} custom-call(bf16[8,128,256]{2,1,0:T(8,128)(2,1)} %bitcast.67, bf16[8,4,576,256]{3,2,1,0:T(8,128)(2,1)} %bitcast.61), custom_call_target="tpu_custom_call" | custom-call | flops 536870912 | bytes 4194304 | tf_op jit(solution)/shard_map/pallas_call | solution.py:145
  143.0 4.8 %shard_map.166 = bf16[112,1024]{1,0:T(8,128)(2,1)} custom-call(bf16[112,2560]{1,0:T(8,128)(2,1)} %maximum_bitcast_fusion.left_ref, bf16[8,4,576,256]{3,2,1,0:T(8,128)(2,1)} %bitcast.62, bf16[8,4,576,256]{3,2,1,0:T(8,128)(2,1)} %bitcast.63, f32[1,1024]{1,0:T(1,128)} %bitcast.91), custom_call_target="tpu_custom_call" | custom-call | flops 587202560 | bytes 5242880 | tf_op jit(solution)/shard_map/pallas_call | solution.py:88
  147.8 2.4 %multiply_reduce_fusion.2 = (f32[128]{0:T(128)S(1)}, f32[128]{0:T(128)S(1)}, bf16[128,1024]{1,0:T(8,128)(2,1)}, f32[128,1024]{1,0:T(8,128)}) fusion(f32[128,1024]{1,0:T(8,128)} %shard_map.167, f32[1024]{0:T(1024)S(1)} %copy-done.6, bf16[1,128,1024]{2,1,0:T(8,128)(2,1)S(1)} %copy-done.3, bf16[112,1024]{1,0:T(8,128)(2,1)} %shard_map.166, ...), kind=kOutput, calls=%fused_computation.24 | convolution fusion | flops 30568192 | bytes 1808048 | tf_op jit(solution)/shard_map/dot_general | solution.py:287
  150.9 3.3 %all-to-all-start.5 = ((f32[8,2,128]{2,1,0:T(2,128)}), f32[8,2,128]{2,1,0:T(2,128)S(1)}, u32[]{:S(2)}, u32[]{:S(2)}) async-start(f32[8,2,128]{2,1,0:T(2,128)} %broadcast_in_dim.40), calls=%async_computation.5 | async-start | bytes 16384 | tf_op jit(solution)/shard_map/all_to_all | solution.py:199
  154.5 6.8 %shard_map.168 = f32[8,128,256]{2,1,0:T(8,128)} custom-call(s32[1]{0:T(128)} %bitcast.36.plane_ref, bf16[128,1024]{1,0:T(8,128)(2,1)} %get-tuple-element.36.left_ref, bf16[8,4,576,256]{3,2,1,0:T(8,128)(2,1)} %bitcast.64), custom_call_target="tpu_custom_call" | custom-call | flops 536870912 | bytes 4194304 | tf_op jit(solution)/shard_map/pallas_call | solution.py:113
  161.2 0.7 all-to-all-done.5
  162.0 2.2 multiply_convert_fusion
  164.2 1.1 reshape.127
  165.5 19.5 %all_to_all.41.normed_ref = bf16[8,128,512]{2,1,0:T(8,128)(2,1)} all-to-all(bf16[8,128,512]{2,1,0:T(8,128)(2,1)S(1)} %bitcast.68), channel_id=1, replica_groups={{0,8,128,136,16,24,144,152},{32,40,160,168,48,56,176,184},{64,72,192,20..., dimensions={0} | all-to-all | bytes 2097152 | tf_op jit(solution)/shard_map/all_to_all | solution.py:304
  185.0 3.1 %shard_map.169 = bf16[4,256,256]{2,1,0:T(8,128)(2,1)} custom-call(bf16[8,128,512]{2,1,0:T(8,128)(2,1)} %all_to_all.41.normed_ref, bf16[8,128,512]{2,1,0:T(8,128)(2,1)} %all-to-all-done.4.cot_ref), custom_call_target="tpu_custom_call" | custom-call | flops 536870912 | bytes 3145728 | tf_op jit(solution)/shard_map/pallas_call | solution.py:173
  188.1 6.4 %all-to-all-start.7 = ((bf16[4,256,256]{2,1,0:T(8,128)(2,1)}), bf16[4,256,256]{2,1,0:T(8,128)(2,1)}, u32[]{:S(2)}, u32[]{:S(2)}) async-start(bf16[4,256,256]{2,1,0:T(8,128)(2,1)} %shard_map.169), calls=%async_computation.8 | async-start | bytes 1048576 | tf_op jit(solution)/shard_map/all_to_all | solution.py:312
  194.5 1.0 convolution_convert_fusion
  195.4 1.5 collective-permute-start.3
  196.9 5.0 %all-to-all-done.7 = bf16[4,256,256]{2,1,0:T(8,128)(2,1)} async-done(((bf16[4,256,256]{2,1,0:T(8,128)(2,1)}), bf16[4,256,256]{2,1,0:T(8,128)(2,1)}, u32[]{:S(2)}, u32[]{:S(2)}) %all-to-all-start.7) | async-done | bytes 524320 | tf_op jit(solution)/shard_map/all_to_all | solution.py:312
  201.9 1.8 reduce_sum.62
  203.7 5.0 %collective-permute-start.4 = (bf16[256,256]{1,0:T(8,128)(2,1)}, bf16[256,256]{1,0:T(8,128)(2,1)S(1)}, u32[]{:S(2)}, u32[]{:S(2)}) collective-permute-start(bf16[256,256]{1,0:T(8,128)(2,1)} %reduce_sum.62), channel_id=1, source_target_pairs={{0,0},{1,33},{2,66},{3,99},{4,132},{5,165},{6,198},{7,231},{8,16},... | collective-permute-start | bytes 393224 | tf_op jit(solution)/shard_map/ppermute | solution.py:314
  208.7 10.0 %collective-permute-done.4 = bf16[256,256]{1,0:T(8,128)(2,1)S(1)} collective-permute-done((bf16[256,256]{1,0:T(8,128)(2,1)}, bf16[256,256]{1,0:T(8,128)(2,1)S(1)}, u32[]{:S(2)}, u32[]{:S(2)}) %collective-permute-start.4) | collective-permute-done | bytes 131104 | tf_op jit(solution)/shard_map/ppermute | solution.py:314
  218.7 0.7 convert_element_type.45
  219.5 1.6 multiply_convert_fusion.2
  221.1 0.7 copy.64
  (62 shorter events, 5.1 us)
Async XLA Ops:
  7.2 82.8 %copy-start = (bf16[5120,320]{0,1:T(8,128)(2,1)S(1)}, bf16[5120,320]{0,1:T(8,128)(2,1)}, u32[]{:S(2)}) copy-start(bf16[5120,320]{0,1:T(8,128)(2,1)} %param.20) | copy-start | bytes 9830404
  7.2 77.1 %all-gather.4.cloned.1.call-start = ((), (), s32[]{:S(2)}) async-start(), calls=%async_computation.9 | async-start | bytes 1474560 | tf_op jit(solution)/shard_map/all_gather | solution.py:231
  9.1 37.5 %copy-start.4 = (bf16[1176,40]{0,1:T(8,128)(2,1)S(1)}, bf16[1176,40]{0,1:T(8,128)(2,1)}, u32[]{:S(2)}) copy-start(bf16[1176,40]{0,1:T(8,128)(2,1)} %param.17) | copy-start | bytes 282244
  13.3 31.6 %all-to-all-start = ((bf16[8,40,256]{2,1,0:T(8,128)(2,1)}), bf16[8,40,256]{2,1,0:T(8,128)(2,1)S(1)}, u32[]{:S(2)}, u32[]{:S(2)}) async-start(bf16[8,40,256]{2,1,0:T(8,128)(2,1)} %shard_map.165), calls=%async_computation | async-start | bytes 327680 | tf_op jit(solution)/shard_map/all_to_all | solution.py:199
  21.8 116.3 %all-gather.6.cloned.1.call-start = ((), (), s32[]{:S(2)}) async-start(), calls=%async_computation.11 | async-start | bytes 9732096 | tf_op jit(solution)/shard_map/all_gather | solution.py:246
  21.8 23.1 %collective-permute-start.2 = (bf16[256,256]{1,0:T(8,128)(2,1)}, bf16[256,256]{1,0:T(8,128)(2,1)}, u32[]{:S(2)}, u32[]{:S(2)}) collective-permute-start(bf16[256,256]{1,0:T(8,128)(2,1)} %param.26), channel_id=1, source_target_pairs={{0,0},{1,32},{2,64},{3,96},{4,128},{5,160},{6,192},{7,224},{8,8},{... | collective-permute-start | bytes 393224 | tf_op jit(solution)/shard_map/ppermute | solution.py:234
  46.5 27.1 %copy-start.5 = (bf16[1,128,256]{2,1,0:T(8,128)(2,1)S(1)}, bf16[1,128,256]{2,1,0:T(8,128)(2,1)}, u32[]{:S(2)}) copy-start(bf16[1,128,256]{2,1,0:T(8,128)(2,1)} %param.27) | copy-start | bytes 196612
  73.6 6.4 %collective-permute-start = (bf16[16,40,1176]{2,1,0:T(8,128)(2,1)}, bf16[16,40,1176]{2,1,0:T(8,128)(2,1)}, u32[]{:S(2)}, u32[]{:S(2)}) collective-permute-start(bf16[16,40,1176]{2,1,0:T(8,128)(2,1)} %all_to_all.40), channel_id=1, source_target_pairs={{0,8},{8,0},{16,24},{24,16},{32,40},{40,32},{48,56},{56,48},{64,72... | collective-permute-start | bytes 4515848 | tf_op jit(solution)/shard_map/ppermute | solution.py:30
  74.4 23.9 %all-to-all-start.2 = ((bf16[8,128,256]{2,1,0:T(8,128)(2,1)}), bf16[8,128,256]{2,1,0:T(8,128)(2,1)}, u32[]{:S(2)}, u32[]{:S(2)}) async-start(bf16[8,128,256]{2,1,0:T(8,128)(2,1)} %broadcast_in_dim.35), calls=%async_computation.2 | async-start | bytes 1048576 | tf_op jit(solution)/shard_map/all_to_all | solution.py:199
  88.6 0.7 copy-start.7
  88.7 0.7 copy-start.8
  89.4 0.7 copy-start.10
  90.0 16.5 %copy-start.11 = (s32[32]{0:T(128)S(1)}, s32[32]{0:T(128)}, u32[]{:S(2)}) copy-start(s32[32]{0:T(128)} %param.15) | copy-start | bytes 388
  91.6 6.8 %collective-permute-start.1 = (bf16[112,320]{1,0:T(8,128)(2,1)S(1)}, bf16[112,320]{1,0:T(8,128)(2,1)S(1)}, u32[]{:S(2)}, u32[]{:S(2)}) collective-permute-start(bf16[112,320]{1,0:T(8,128)(2,1)S(1)} %reshape.118), channel_id=1, source_target_pairs={{0,128},{128,0},{1,129},{129,1},{2,130},{130,2},{3,131},{131,3},{4... | collective-permute-start | bytes 215048 | tf_op jit(solution)/shard_map/ppermute | solution.py:34
  99.4 27.0 %all-to-all-start.3 = ((bf16[8,320,112]{2,1,0:T(8,128)(2,1)}), bf16[8,320,112]{2,1,0:T(8,128)(2,1)}, u32[]{:S(2)}, u32[]{:S(2)}) async-start(bf16[8,320,112]{2,1,0:T(8,128)(2,1)} %broadcast_in_dim.38), calls=%async_computation.3 | async-start | bytes 1310720 | tf_op jit(solution)/shard_map/all_to_all | solution.py:199
  109.4 0.8 copy-start.1
  110.8 21.2 %copy-start.9 = (s32[1,112]{1,0:T(1,128)S(1)}, s32[1,112]{1,0:T(1,128)}, u32[]{:S(2)}) copy-start(s32[1,112]{1,0:T(1,128)} %param.16) | copy-start | bytes 1348
  126.4 23.8 %all-to-all-start.4 = ((bf16[8,128,512]{2,1,0:T(8,128)(2,1)}), bf16[8,128,512]{2,1,0:T(8,128)(2,1)}, u32[]{:S(2)}, u32[]{:S(2)}) async-start(bf16[8,128,512]{2,1,0:T(8,128)(2,1)} %reshape.120), calls=%async_computation.4 | async-start | bytes 2097152 | tf_op jit(solution)/shard_map/all_to_all | solution.py:274
  143.0 4.8 %copy-start.3 = (bf16[1,128,1024]{2,1,0:T(8,128)(2,1)S(1)}, bf16[1,128,1024]{2,1,0:T(8,128)(2,1)}, u32[]{:S(2)}) copy-start(bf16[1,128,1024]{2,1,0:T(8,128)(2,1)} %param.24) | copy-start | bytes 786436
  143.0 4.8 %copy-start.6 = (f32[1024]{0:T(1024)S(1)}, f32[1024]{0:T(1024)}, u32[]{:S(2)}) copy-start(f32[1024]{0:T(1024)} %param.25) | copy-start | bytes 12292
  150.9 11.0 %all-to-all-start.5 = ((f32[8,2,128]{2,1,0:T(2,128)}), f32[8,2,128]{2,1,0:T(2,128)S(1)}, u32[]{:S(2)}, u32[]{:S(2)}) async-start(f32[8,2,128]{2,1,0:T(2,128)} %broadcast_in_dim.40), calls=%async_computation.5 | async-start | bytes 16384 | tf_op jit(solution)/shard_map/all_to_all | solution.py:199
  154.2 65.2 %reduce-scatter.2.cloned.1.call-start = ((), (), s32[]{:S(2)}) async-start(), calls=%async_computation.10 | async-start | bytes 1179648 | tf_op jit(solution)/shard_map/reduce_scatter | solution.py:316
  165.5 29.0 %copy-start.2 = (bf16[128,1024]{1,0:T(8,128)(2,1)S(1)}, bf16[128,1024]{1,0:T(8,128)(2,1)}, u32[]{:S(2)}) copy-start(bf16[128,1024]{1,0:T(8,128)(2,1)} %get-tuple-element.35) | copy-start | bytes 786436
  188.1 13.8 %all-to-all-start.7 = ((bf16[4,256,256]{2,1,0:T(8,128)(2,1)}), bf16[4,256,256]{2,1,0:T(8,128)(2,1)}, u32[]{:S(2)}, u32[]{:S(2)}) async-start(bf16[4,256,256]{2,1,0:T(8,128)(2,1)} %shard_map.169), calls=%async_computation.8 | async-start | bytes 1048576 | tf_op jit(solution)/shard_map/all_to_all | solution.py:312
  195.4 13.3 %collective-permute-start.3 = (bf16[112,1024]{1,0:T(8,128)(2,1)}, bf16[112,1024]{1,0:T(8,128)(2,1)S(1)}, u32[]{:S(2)}, u32[]{:S(2)}) collective-permute-start(bf16[112,1024]{1,0:T(8,128)(2,1)} %convolution_convert_fusion), channel_id=1, source_target_pairs={{0,128},{128,0},{1,129},{129,1},{2,130},{130,2},{3,131},{131,3},{4... | collective-permute-start | bytes 688136 | tf_op jit(solution)/shard_map/ppermute | solution.py:34
  203.7 15.0 %collective-permute-start.4 = (bf16[256,256]{1,0:T(8,128)(2,1)}, bf16[256,256]{1,0:T(8,128)(2,1)S(1)}, u32[]{:S(2)}, u32[]{:S(2)}) collective-permute-start(bf16[256,256]{1,0:T(8,128)(2,1)} %reduce_sum.62), channel_id=1, source_target_pairs={{0,0},{1,33},{2,66},{3,99},{4,132},{5,165},{6,198},{7,231},{8,16},... | collective-permute-start | bytes 393224 | tf_op jit(solution)/shard_map/ppermute | solution.py:314
Sparse Core Ops, SparseCore 0:
  10.4 48.7 all-gather.3
  61.1 71.5 all-gather.5
  162.1 38.8 reduce-scatter.1

commit v5 on v4

--- a/solution.py
+++ b/solution.py
@@ -53,26 +53,6 @@
                     row = 4 * t + 2 * core + x // 2
                     route.append((source, row * N_TP + ((2 * y + x % 2) ^ t)))
     return route
-
-
-def share_kernel(place_ref, block_ref, out_ref):
-    out_ref[0] = block_ref[...]
-
-
-def take_share(weight, place):
-    return pl.pallas_call(
-        share_kernel,
-        grid_spec=pltpu.PrefetchScalarGridSpec(
-            num_scalar_prefetch=1,
-            grid=(N_TP,),
-            in_specs=[
-                pl.BlockSpec((40, 256), lambda i, place: (place[0] // 4, 4 * i + place[0] % 4))
-            ],
-            out_specs=pl.BlockSpec((1, 40, 256), lambda i, place: (i, 0, 0)),
-        ),
-        out_shape=jax.ShapeDtypeStruct((N_TP, 40, 256), BF),
-        cost_estimate=pl.CostEstimate(flops=0, bytes_accessed=640 * 512, transcendentals=0),
-    )(place.astype(jnp.int32)[None], weight)
 
 
 def vision_kernel(left_ref, most_ref, rest_ref, bias_ref, out_ref):
@@ -232,7 +212,10 @@
 
     place = sec * 16 + dp
     weight_block = lax.ppermute(kv_weight, ALL, weight_to_plane())
-    share = exchange_tp(take_share(w_out, place)).reshape(320, 256)
+    share = lax.dynamic_slice_in_dim(w_out, place // 4 * 40, 40, axis=0)
+    share = share.reshape(40, N_TP, 4, 256)
+    share = lax.dynamic_index_in_dim(share, place % 4, axis=2, keepdims=False).transpose(1, 0, 2)
+    share = exchange_tp(share).reshape(320, 256)
 
     columns, _ = lax.optimization_barrier((pe_weight.T, share))
     mine = lax.all_to_all(

time: 232 us -> 235 us (1.013)
  local copies, waits for them, and re-layouts: 17.1 us -> 24.1 us
  Pallas kernels: 23.8 us -> 19.6 us
    pallas_call x1 -> x0, Pallas kernels: 4.21 us -> none  [take_share(): pl.pallas_call(share_kernel, grid_spec=pltpu.PrefetchScalarGridSpec(num_s...]
    dynamic_slice x0 -> x3, local copies, waits for them, and re-layouts: none -> 4.17 us  [the longest x2 2.19 us: per_device(): lax.dynamic_index_in_dim(share, place % 4, axis=2, keepdims=False)]
    reshape x0 -> x1, local copies, waits for them, and re-layouts: none -> 2.72 us  [per_device(): share = share.reshape(40, N_TP, 4, 256)]
  transfers between devices with their start and end apart: 14 -> 14, of which waited for: 6 -> 7; matrix products, arithmetic and copies ran while one was open for 16% -> 19% of each run, Pallas kernels for 10% -> 8%
where the time goes in v5:
time: 235 us; the launch traced here: 232 us
  waiting for transfers between devices  51.7 us (22%)
  starting transfers between devices  48.7 us (21%)
  blocking collectives  47 us (20%)
  local copies, waits for them, and re-layouts  24.1 us (10%)
  Pallas kernels  19.6 us (8%)
  other arithmetic  17.3 us (7%)
  between operations  14.1 us (6%)
  matrix products  9.1 us (4%)
    all_to_all x1, blocking collectives, per_device(): lax.all_to_all(jnp.broadcast_to(columns[None], (16,) + columns.shape), PL...  27.6 us
    all_to_all x4, starting transfers between devices, exchange_tp(): return lax.all_to_all(blocks, 'tp', 0, 0)  24.3 us
    all_to_all x1, blocking collectives, per_device(): lax.all_to_all(jnp.broadcast_to(normed[None], (4, 2, 128, 512)).reshape(8...  19.5 us
    ppermute x1, waiting for transfers between devices, per_device(): weight_block = lax.ppermute(kv_weight, ALL, weight_to_plane())  18.5 us
    all_to_all x4, waiting for transfers between devices, exchange_tp(): return lax.all_to_all(blocks, 'tp', 0, 0)  17.7 us
    ppermute x1, waiting for transfers between devices, per_device(): kv_weight_grad = lax.ppermute(block, ALL, grad_from_plane()).astype(F32)  10 us
    pallas_call x1, Pallas kernels, block_product(): pl.pallas_call(block_product_kernel, grid_spec=pltpu.PrefetchScalarGridSp...  6.76 us
    all_to_all x1, starting transfers between devices, per_device(): block = lax.all_to_all(block, PLANE, 0, 0, axis_index_groups=SAME_Y)  5.77 us
  transfers between devices with their start and end apart: 14, of which 7 were waited for; matrix products, arithmetic and copies ran while one was open for 19% of the time, Pallas kernels for 8%

profile of v5, /device:TPU:14, one launch (start us, length us, event | category | flops | bytes accessed | tf_op | source)
XLA Modules:
  0.0 231.7 jit_solution(627734929505120718)
XLA Ops:
  7.2 1.1 reshape_squeeze.15
  9.1 2.0 constant_dynamic-slice_fusion.1
  11.1 2.7 %reshape.117 = bf16[40,8,4,256]{3,2,1,0:T(4,128)(2,1)} reshape(bf16[40,8192]{1,0:T(8,128)(2,1)} %constant_dynamic-slice_fusion.1) | data formatting | bytes 1310720 | tf_op jit(solution)/shard_map/reshape | solution.py:216
  13.8 1.4 constant_dynamic-slice_fusion
  15.2 0.8 copy.69
  16.0 8.5 %all-to-all-start = ((bf16[8,40,256]{2,1,0:T(8,128)(2,1)}), bf16[8,40,256]{2,1,0:T(8,128)(2,1)S(1)}, u32[]{:S(2)}, u32[]{:S(2)}) async-start(bf16[8,40,256]{2,1,0:T(8,128)(2,1)} %bitcast.82), calls=%async_computation | async-start | bytes 327680 | tf_op jit(solution)/shard_map/all_to_all | solution.py:179
  24.5 5.1 %collective-permute-start.2 = (bf16[256,256]{1,0:T(8,128)(2,1)}, bf16[256,256]{1,0:T(8,128)(2,1)}, u32[]{:S(2)}, u32[]{:S(2)}) collective-permute-start(bf16[256,256]{1,0:T(8,128)(2,1)} %param.26), channel_id=1, source_target_pairs={{0,0},{1,32},{2,64},{3,96},{4,128},{5,160},{6,192},{7,224},{8,8},{... | collective-permute-start | bytes 393224 | tf_op jit(solution)/shard_map/ppermute | solution.py:214
  29.6 18.5 %collective-permute-done.2 = bf16[256,256]{1,0:T(8,128)(2,1)} collective-permute-done((bf16[256,256]{1,0:T(8,128)(2,1)}, bf16[256,256]{1,0:T(8,128)(2,1)}, u32[]{:S(2)}, u32[]{:S(2)}) %collective-permute-start.2) | collective-permute-done | bytes 131104 | tf_op jit(solution)/shard_map/ppermute | solution.py:214
  48.1 1.6 pad_maximum_fusion.1
  49.9 27.6 %all_to_all.40 = bf16[16,40,1176]{2,1,0:T(8,128)(2,1)} all-to-all(bf16[16,40,1176]{2,1,0:T(8,128)(2,1)S(1)} %broadcast_in_dim.31), channel_id=1, replica_groups={{0,16,32,48,64,80,96,112,128,144,160,176,192,208,224,240},{8,24,40,56,7..., dimensions={0} | all-to-all | bytes 3010560 | tf_op jit(solution)/shard_map/all_to_all | solution.py:221
  77.5 0.8 broadcast_in_dim.32
  78.3 5.4 %all-to-all-start.2 = ((bf16[8,128,256]{2,1,0:T(8,128)(2,1)}), bf16[8,128,256]{2,1,0:T(8,128)(2,1)}, u32[]{:S(2)}, u32[]{:S(2)}) async-start(bf16[8,128,256]{2,1,0:T(8,128)(2,1)} %broadcast_in_dim.32), calls=%async_computation.2 | async-start | bytes 1048576 | tf_op jit(solution)/shard_map/all_to_all | solution.py:179
  83.7 2.2 select_bitcast_fusion.1
  85.9 2.0 pad_maximum_fusion
  87.9 4.4 %fusion.33 = (f32[512]{0:T(512)S(1)}, f32[512,1280]{1,0:T(8,128)S(1)}) fusion(bf16[512,1176]{1,0:T(8,128)(2,1)} %all-gather.4.cloned.1.call-done, bf16[1280,1176]{1,0:T(8,128)(2,1)} %bitcast.73), kind=kOutput, calls=%fused_computation.65 | convolution fusion | flops 1542061568 | bytes 6838272 | tf_op jit(solution)/shard_map/dot_general | solution.py:237
  93.7 1.3 fusion.13
  95.2 1.7 collective-permute-start.1
  96.9 5.1 %all-to-all-done.2 = bf16[8,128,256]{2,1,0:T(8,128)(2,1)} async-done(((bf16[8,128,256]{2,1,0:T(8,128)(2,1)}), bf16[8,128,256]{2,1,0:T(8,128)(2,1)}, u32[]{:S(2)}, u32[]{:S(2)}) %all-to-all-start.2) | async-done | bytes 524320 | tf_op jit(solution)/shard_map/all_to_all | solution.py:179
  102.2 1.0 broadcast_in_dim.35
  103.2 7.1 %all-to-all-start.3 = ((bf16[8,320,112]{2,1,0:T(8,128)(2,1)}), bf16[8,320,112]{2,1,0:T(8,128)(2,1)}, u32[]{:S(2)}, u32[]{:S(2)}) async-start(bf16[8,320,112]{2,1,0:T(8,128)(2,1)} %broadcast_in_dim.35), calls=%async_computation.3 | async-start | bytes 1310720 | tf_op jit(solution)/shard_map/all_to_all | solution.py:179
  111.5 1.4 reverse_select_fusion.2
  113.1 0.8 copy-done.1
  114.5 1.5 broadcast_in_dim.34
  116.0 2.5 %reshape.124 = bf16[8,128,512]{2,1,0:T(8,128)(2,1)} reshape(bf16[4,2,128,2,256]{4,3,2,1,0:T(2,128)(2,1)} %broadcast_in_dim.34) | data formatting | bytes 2097152 | tf_op jit(solution)/shard_map/reshape | solution.py:255
  118.6 11.8 %all-to-all-done.3 = bf16[8,320,112]{2,1,0:T(8,128)(2,1)} async-done(((bf16[8,320,112]{2,1,0:T(8,128)(2,1)}), bf16[8,320,112]{2,1,0:T(8,128)(2,1)}, u32[]{:S(2)}, u32[]{:S(2)}) %all-to-all-start.3) | async-done | bytes 573472 | tf_op jit(solution)/shard_map/all_to_all | solution.py:179
  130.3 5.6 %all-to-all-start.4 = ((bf16[8,128,512]{2,1,0:T(8,128)(2,1)}), bf16[8,128,512]{2,1,0:T(8,128)(2,1)}, u32[]{:S(2)}, u32[]{:S(2)}) async-start(bf16[8,128,512]{2,1,0:T(8,128)(2,1)} %reshape.124), calls=%async_computation.4 | async-start | bytes 2097152 | tf_op jit(solution)/shard_map/all_to_all | solution.py:257
  136.0 1.2 copy.56
  137.2 0.8 slice.41
  138.0 2.0 copy.61
  140.2 1.9 maximum_bitcast_fusion.left_ref
  142.0 4.9 %shard_map.166 = f32[128,1024]{1,0:T(8,128)} custom-call(bf16[8,128,256]{2,1,0:T(8,128)(2,1)} %bitcast.71, bf16[8,4,576,256]{3,2,1,0:T(8,128)(2,1)} %bitcast.65), custom_call_target="tpu_custom_call" | custom-call | flops 536870912 | bytes 4194304 | tf_op jit(solution)/shard_map/pallas_call | solution.py:125
  147.0 4.8 %shard_map.165 = bf16[112,1024]{1,0:T(8,128)(2,1)} custom-call(bf16[112,2560]{1,0:T(8,128)(2,1)} %maximum_bitcast_fusion.left_ref, bf16[8,4,576,256]{3,2,1,0:T(8,128)(2,1)} %bitcast.66, bf16[8,4,576,256]{3,2,1,0:T(8,128)(2,1)} %bitcast.67, f32[1,1024]{1,0:T(1,128)} %bitcast.96), custom_call_target="tpu_custom_call" | custom-call | flops 587202560 | bytes 5242880 | tf_op jit(solution)/shard_map/pallas_call | solution.py:68
  151.8 2.4 %multiply_reduce_fusion.2 = (f32[128]{0:T(128)S(1)}, f32[128]{0:T(128)S(1)}, bf16[128,1024]{1,0:T(8,128)(2,1)}, f32[128,1024]{1,0:T(8,128)}) fusion(f32[128,1024]{1,0:T(8,128)} %shard_map.166, f32[1024]{0:T(1024)S(1)} %copy-done.6, bf16[1,128,1024]{2,1,0:T(8,128)(2,1)S(1)} %copy-done.3, bf16[112,1024]{1,0:T(8,128)(2,1)} %shard_map.165, ...), kind=kOutput, calls=%fused_computation.24 | convolution fusion | flops 30568192 | bytes 1808048 | tf_op jit(solution)/shard_map/dot_general | solution.py:270
  154.9 3.3 %all-to-all-start.5 = ((f32[8,2,128]{2,1,0:T(2,128)}), f32[8,2,128]{2,1,0:T(2,128)S(1)}, u32[]{:S(2)}, u32[]{:S(2)}) async-start(f32[8,2,128]{2,1,0:T(2,128)} %broadcast_in_dim.37), calls=%async_computation.5 | async-start | bytes 16384 | tf_op jit(solution)/shard_map/all_to_all | solution.py:179
  158.3 6.8 %shard_map.167 = f32[8,128,256]{2,1,0:T(8,128)} custom-call(s32[1]{0:T(128)} %bitcast.37.plane_ref, bf16[128,1024]{1,0:T(8,128)(2,1)} %get-tuple-element.36.left_ref, bf16[8,4,576,256]{3,2,1,0:T(8,128)(2,1)} %bitcast.68), custom_call_target="tpu_custom_call" | custom-call | flops 536870912 | bytes 4194304 | tf_op jit(solution)/shard_map/pallas_call | solution.py:93
  165.0 0.9 all-to-all-done.5
  166.0 2.2 multiply_convert_fusion
  168.2 1.1 reshape.131
  169.5 19.5 %all_to_all.41.normed_ref = bf16[8,128,512]{2,1,0:T(8,128)(2,1)} all-to-all(bf16[8,128,512]{2,1,0:T(8,128)(2,1)S(1)} %bitcast.72), channel_id=1, replica_groups={{0,8,128,136,16,24,144,152},{32,40,160,168,48,56,176,184},{64,72,192,20..., dimensions={0} | all-to-all | bytes 2097152 | tf_op jit(solution)/shard_map/all_to_all | solution.py:287
  189.0 3.1 %shard_map.168 = bf16[4,256,256]{2,1,0:T(8,128)(2,1)} custom-call(bf16[8,128,512]{2,1,0:T(8,128)(2,1)} %all_to_all.41.normed_ref, bf16[8,128,512]{2,1,0:T(8,128)(2,1)} %all-to-all-done.4.cot_ref), custom_call_target="tpu_custom_call" | custom-call | flops 536870912 | bytes 3145728 | tf_op jit(solution)/shard_map/pallas_call | solution.py:153
  192.1 5.8 %all-to-all-start.7 = ((bf16[4,256,256]{2,1,0:T(8,128)(2,1)}), bf16[4,256,256]{2,1,0:T(8,128)(2,1)}, u32[]{:S(2)}, u32[]{:S(2)}) async-start(bf16[4,256,256]{2,1,0:T(8,128)(2,1)} %shard_map.168), calls=%async_computation.8 | async-start | bytes 1048576 | tf_op jit(solution)/shard_map/all_to_all | solution.py:295
  197.9 0.9 convolution_convert_fusion
  198.8 1.4 collective-permute-start.3
  200.3 5.3 %all-to-all-done.7 = bf16[4,256,256]{2,1,0:T(8,128)(2,1)} async-done(((bf16[4,256,256]{2,1,0:T(8,128)(2,1)}), bf16[4,256,256]{2,1,0:T(8,128)(2,1)}, u32[]{:S(2)}, u32[]{:S(2)}) %all-to-all-start.7) | async-done | bytes 524320 | tf_op jit(solution)/shard_map/all_to_all | solution.py:295
  205.6 1.8 reduce_sum.62
  207.4 4.7 %collective-permute-start.4 = (bf16[256,256]{1,0:T(8,128)(2,1)}, bf16[256,256]{1,0:T(8,128)(2,1)S(1)}, u32[]{:S(2)}, u32[]{:S(2)}) collective-permute-start(bf16[256,256]{1,0:T(8,128)(2,1)} %reduce_sum.62), channel_id=1, source_target_pairs={{0,0},{1,33},{2,66},{3,99},{4,132},{5,165},{6,198},{7,231},{8,16},... | collective-permute-start | bytes 393224 | tf_op jit(solution)/shard_map/ppermute | solution.py:297
  212.1 10.0 %collective-permute-done.4 = bf16[256,256]{1,0:T(8,128)(2,1)S(1)} collective-permute-done((bf16[256,256]{1,0:T(8,128)(2,1)}, bf16[256,256]{1,0:T(8,128)(2,1)S(1)}, u32[]{:S(2)}, u32[]{:S(2)}) %collective-permute-start.4) | collective-permute-done | bytes 131104 | tf_op jit(solution)/shard_map/ppermute | solution.py:297
  222.8 1.6 multiply_convert_fusion.2
  (65 shorter events, 7.2 us)
Async XLA Ops:
  7.2 86.5 %copy-start = (bf16[5120,320]{0,1:T(8,128)(2,1)S(1)}, bf16[5120,320]{0,1:T(8,128)(2,1)}, u32[]{:S(2)}) copy-start(bf16[5120,320]{0,1:T(8,128)(2,1)} %param.20) | copy-start | bytes 9830404
  7.2 80.7 %all-gather.4.cloned.1.call-start = ((), (), s32[]{:S(2)}) async-start(), calls=%async_computation.9 | async-start | bytes 1474560 | tf_op jit(solution)/shard_map/all_gather | solution.py:211
  9.0 40.8 %copy-start.4 = (bf16[1176,40]{0,1:T(8,128)(2,1)S(1)}, bf16[1176,40]{0,1:T(8,128)(2,1)}, u32[]{:S(2)}) copy-start(bf16[1176,40]{0,1:T(8,128)(2,1)} %param.17) | copy-start | bytes 282244
  16.0 32.1 %all-to-all-start = ((bf16[8,40,256]{2,1,0:T(8,128)(2,1)}), bf16[8,40,256]{2,1,0:T(8,128)(2,1)S(1)}, u32[]{:S(2)}, u32[]{:S(2)}) async-start(bf16[8,40,256]{2,1,0:T(8,128)(2,1)} %bitcast.82), calls=%async_computation | async-start | bytes 327680 | tf_op jit(solution)/shard_map/all_to_all | solution.py:179
  24.5 117.6 %all-gather.6.cloned.1.call-start = ((), (), s32[]{:S(2)}) async-start(), calls=%async_computation.11 | async-start | bytes 9732096 | tf_op jit(solution)/shard_map/all_gather | solution.py:229
  24.5 23.6 %collective-permute-start.2 = (bf16[256,256]{1,0:T(8,128)(2,1)}, bf16[256,256]{1,0:T(8,128)(2,1)}, u32[]{:S(2)}, u32[]{:S(2)}) collective-permute-start(bf16[256,256]{1,0:T(8,128)(2,1)} %param.26), channel_id=1, source_target_pairs={{0,0},{1,32},{2,64},{3,96},{4,128},{5,160},{6,192},{7,224},{8,8},{... | collective-permute-start | bytes 393224 | tf_op jit(solution)/shard_map/ppermute | solution.py:214
  49.8 27.7 %copy-start.5 = (bf16[1,128,256]{2,1,0:T(8,128)(2,1)S(1)}, bf16[1,128,256]{2,1,0:T(8,128)(2,1)}, u32[]{:S(2)}) copy-start(bf16[1,128,256]{2,1,0:T(8,128)(2,1)} %param.27) | copy-start | bytes 196612
  77.5 6.2 %collective-permute-start = (bf16[16,40,1176]{2,1,0:T(8,128)(2,1)}, bf16[16,40,1176]{2,1,0:T(8,128)(2,1)}, u32[]{:S(2)}, u32[]{:S(2)}) collective-permute-start(bf16[16,40,1176]{2,1,0:T(8,128)(2,1)} %all_to_all.40), channel_id=1, source_target_pairs={{0,8},{8,0},{16,24},{24,16},{32,40},{40,32},{48,56},{56,48},{64,72... | collective-permute-start | bytes 4515848 | tf_op jit(solution)/shard_map/ppermute | solution.py:30
  78.3 23.7 %all-to-all-start.2 = ((bf16[8,128,256]{2,1,0:T(8,128)(2,1)}), bf16[8,128,256]{2,1,0:T(8,128)(2,1)}, u32[]{:S(2)}, u32[]{:S(2)}) async-start(bf16[8,128,256]{2,1,0:T(8,128)(2,1)} %broadcast_in_dim.32), calls=%async_computation.2 | async-start | bytes 1048576 | tf_op jit(solution)/shard_map/all_to_all | solution.py:179
  92.3 0.7 copy-start.7
  92.3 0.7 copy-start.8
  93.0 0.7 copy-start.10
  93.7 16.6 %copy-start.11 = (s32[32]{0:T(128)S(1)}, s32[32]{0:T(128)}, u32[]{:S(2)}) copy-start(s32[32]{0:T(128)} %param.15) | copy-start | bytes 388
  95.2 6.9 %collective-permute-start.1 = (bf16[112,320]{1,0:T(8,128)(2,1)S(1)}, bf16[112,320]{1,0:T(8,128)(2,1)S(1)}, u32[]{:S(2)}, u32[]{:S(2)}) collective-permute-start(bf16[112,320]{1,0:T(8,128)(2,1)S(1)} %reshape.122), channel_id=1, source_target_pairs={{0,128},{128,0},{1,129},{129,1},{2,130},{130,2},{3,131},{131,3},{4... | collective-permute-start | bytes 215048 | tf_op jit(solution)/shard_map/ppermute | solution.py:34
  103.2 27.1 %all-to-all-start.3 = ((bf16[8,320,112]{2,1,0:T(8,128)(2,1)}), bf16[8,320,112]{2,1,0:T(8,128)(2,1)}, u32[]{:S(2)}, u32[]{:S(2)}) async-start(bf16[8,320,112]{2,1,0:T(8,128)(2,1)} %broadcast_in_dim.35), calls=%async_computation.3 | async-start | bytes 1310720 | tf_op jit(solution)/shard_map/all_to_all | solution.py:179
  113.1 0.8 copy-start.1
  114.5 21.4 %copy-start.9 = (s32[1,112]{1,0:T(1,128)S(1)}, s32[1,112]{1,0:T(1,128)}, u32[]{:S(2)}) copy-start(s32[1,112]{1,0:T(1,128)} %param.16) | copy-start | bytes 1348
  130.3 24.0 %all-to-all-start.4 = ((bf16[8,128,512]{2,1,0:T(8,128)(2,1)}), bf16[8,128,512]{2,1,0:T(8,128)(2,1)}, u32[]{:S(2)}, u32[]{:S(2)}) async-start(bf16[8,128,512]{2,1,0:T(8,128)(2,1)} %reshape.124), calls=%async_computation.4 | async-start | bytes 2097152 | tf_op jit(solution)/shard_map/all_to_all | solution.py:257
  147.0 4.8 %copy-start.3 = (bf16[1,128,1024]{2,1,0:T(8,128)(2,1)S(1)}, bf16[1,128,1024]{2,1,0:T(8,128)(2,1)}, u32[]{:S(2)}) copy-start(bf16[1,128,1024]{2,1,0:T(8,128)(2,1)} %param.24) | copy-start | bytes 786436
  147.0 4.8 %copy-start.6 = (f32[1024]{0:T(1024)S(1)}, f32[1024]{0:T(1024)}, u32[]{:S(2)}) copy-start(f32[1024]{0:T(1024)} %param.25) | copy-start | bytes 12292
  154.9 11.0 %all-to-all-start.5 = ((f32[8,2,128]{2,1,0:T(2,128)}), f32[8,2,128]{2,1,0:T(2,128)S(1)}, u32[]{:S(2)}, u32[]{:S(2)}) async-start(f32[8,2,128]{2,1,0:T(2,128)} %broadcast_in_dim.37), calls=%async_computation.5 | async-start | bytes 16384 | tf_op jit(solution)/shard_map/all_to_all | solution.py:179
  158.2 64.6 %reduce-scatter.2.cloned.1.call-start = ((), (), s32[]{:S(2)}) async-start(), calls=%async_computation.10 | async-start | bytes 1179648 | tf_op jit(solution)/shard_map/reduce_scatter | solution.py:299
  169.5 28.4 %copy-start.2 = (bf16[128,1024]{1,0:T(8,128)(2,1)S(1)}, bf16[128,1024]{1,0:T(8,128)(2,1)}, u32[]{:S(2)}) copy-start(bf16[128,1024]{1,0:T(8,128)(2,1)} %get-tuple-element.35) | copy-start | bytes 786436
  192.1 13.5 %all-to-all-start.7 = ((bf16[4,256,256]{2,1,0:T(8,128)(2,1)}), bf16[4,256,256]{2,1,0:T(8,128)(2,1)}, u32[]{:S(2)}, u32[]{:S(2)}) async-start(bf16[4,256,256]{2,1,0:T(8,128)(2,1)} %shard_map.168), calls=%async_computation.8 | async-start | bytes 1048576 | tf_op jit(solution)/shard_map/all_to_all | solution.py:295
  198.8 13.3 %collective-permute-start.3 = (bf16[112,1024]{1,0:T(8,128)(2,1)}, bf16[112,1024]{1,0:T(8,128)(2,1)S(1)}, u32[]{:S(2)}, u32[]{:S(2)}) collective-permute-start(bf16[112,1024]{1,0:T(8,128)(2,1)} %convolution_convert_fusion), channel_id=1, source_target_pairs={{0,128},{128,0},{1,129},{129,1},{2,130},{130,2},{3,131},{131,3},{4... | collective-permute-start | bytes 688136 | tf_op jit(solution)/shard_map/ppermute | solution.py:34
  207.4 14.7 %collective-permute-start.4 = (bf16[256,256]{1,0:T(8,128)(2,1)}, bf16[256,256]{1,0:T(8,128)(2,1)S(1)}, u32[]{:S(2)}, u32[]{:S(2)}) collective-permute-start(bf16[256,256]{1,0:T(8,128)(2,1)} %reduce_sum.62), channel_id=1, source_target_pairs={{0,0},{1,33},{2,66},{3,99},{4,132},{5,165},{6,198},{7,231},{8,16},... | collective-permute-start | bytes 393224 | tf_op jit(solution)/shard_map/ppermute | solution.py:297
Sparse Core Ops, SparseCore 0:
  10.4 49.5 all-gather.3
  61.9 71.1 all-gather.5
  166.1 38.8 reduce-scatter.1
